TPU v7x, 256 devices: a whole 4x4x8 slice. The times are simulated.
256 devices in a mesh: ctx: 16 (over z_hi, y), smp: 8 (over x, core), dp: 2 (over z_lo).
Axes of the slice: x: 4, y: 4, z: 8 (z_hi: 4, z_lo: 2; z = z_hi * 2 + z_lo), core: 2. Of those that a mesh axis runs over, the one named last changes fastest.
Arguments:
- queries: bfloat16 [16, 2048, 4096], P(('dp', 'smp'), 'ctx'), parts along dimension 0, may hold values from -64 to 64
- key_prefix: bfloat16 [2048, 512], P(('dp', 'ctx')), parts along dimension 0, may hold values from -16 to 16
- value_prefix: bfloat16 [2048, 512], P(('dp', 'ctx')), parts along dimension 0, may hold values from -6 to 6
- key_response: bfloat16 [16, 2048, 512], P(('dp', 'smp'), 'ctx'), parts along dimension 0, may hold values from -6 to 6
- value_response: bfloat16 [16, 2048, 512], P(('dp', 'smp'), 'ctx'), parts along dimension 0, may hold values from -6 to 6
- output_gradient: bfloat16 [16, 2048, 4096], P(('dp', 'smp'), 'ctx'), parts along dimension 0, may hold values from -6 to 6
- lengths: int32 [32], P('dp'), parts along dimension 0, may hold values from 1 to 1024, as said below
- assign: int32 [32], P('dp'), parts along dimension 0, may hold values from 0 to 7, as said below
Outputs:
- grad_queries: bfloat16 [16, 2048, 4096], P(('dp', 'smp'), 'ctx'), parts along dimension 0
- grad_key_prefix: bfloat16 [2048, 512], P(('dp', 'ctx')), parts along dimension 0
- grad_value_prefix: bfloat16 [2048, 512], P(('dp', 'ctx')), parts along dimension 0
- grad_key_response: bfloat16 [16, 2048, 512], P(('dp', 'smp'), 'ctx'), parts along dimension 0
- grad_value_response: bfloat16 [16, 2048, 512], P(('dp', 'smp'), 'ctx'), parts along dimension 0
There are 2 independent parts, one for each index of `dp`. A program takes and returns all parts, laid end to end along the dimension named above; each array names one. Nothing has to cross between parts.
Inputs may be any that keep to these rules, and one draw needn't show every extreme that they name: One response has exactly 1024 tokens; every other response has 256 to 512 tokens; the lengths on one index of smp sum to at most 2048. `assign`: every index of smp is named by one to three responses.
All inputs are finite; a program needn't handle non-finite values.
Results may differ from a plain program's by a relative error of at most 0.0057.
Values may be sent and summed in bfloat16 or wider, within the bound.
A program may use at most 128 MiB of HBM per device.

v0:
```python
import jax
import jax.numpy as jnp
from jax import lax
from jax.sharding import PartitionSpec as P

QUERY_HEADS = 32
KEY_HEADS = 4
HEAD_SIZE = 128
GROUP_QUERIES = 8


NEG = -1e30


def segment_table(lengths, assign, sample_index, total_slots):
    on_index = (assign == sample_index).astype(jnp.int32)
    spans = lengths * on_index
    ends = jnp.cumsum(spans)
    starts = ends - spans
    slot_ids = jnp.arange(total_slots, dtype=jnp.int32)
    inside = (
        (slot_ids[:, None] >= starts[None, :])
        & (slot_ids[:, None] < ends[None, :])
        & (on_index[None, :] > 0)
    )
    number = jnp.arange(lengths.shape[0], dtype=jnp.int32) + 1
    segs = jnp.sum(inside.astype(jnp.int32) * number[None, :], axis=1) - 1
    return (segs, starts)


def sum_prefix_totals(dk_part, dv_part):
    dk_sum, dv_sum = lax.psum((dk_part, dv_part), "smp")
    return (dk_sum.astype(jnp.bfloat16), dv_sum.astype(jnp.bfloat16))


def shards(
    queries,
    key_prefix,
    value_prefix,
    key_response,
    value_response,
    output_gradient,
    lengths,
    assign,
):
    scale = HEAD_SIZE ** (-0.5)
    count_ctx = lax.axis_size("ctx")
    place = lax.axis_index("ctx")
    token_rows = queries.shape[1]
    kv_width = key_prefix.shape[1]
    total_slots = token_rows * count_ctx
    block = min(512, total_slots)
    seg_all, starts = segment_table(lengths, assign, lax.axis_index("smp"), total_slots)
    first_slot = place * token_rows
    my_slots = first_slot + jnp.arange(token_rows, dtype=jnp.int32)
    seg_rows = lax.dynamic_slice_in_dim(seg_all, first_slot, token_rows)
    live_rows = seg_rows >= 0
    prefix_k, prefix_v = (
        lax.all_gather(key_prefix, "ctx", axis=0, tiled=True),
        lax.all_gather(value_prefix, "ctx", axis=0, tiled=True),
    )
    resp_k, resp_v = (
        lax.all_gather(key_response[0], "ctx", axis=0, tiled=True),
        lax.all_gather(value_response[0], "ctx", axis=0, tiled=True),
    )
    query_head_split = queries[0].reshape(token_rows, KEY_HEADS, GROUP_QUERIES, HEAD_SIZE)
    output_gradient_heads = output_gradient[0].reshape(
        token_rows, KEY_HEADS, GROUP_QUERIES, HEAD_SIZE
    )
    prefix_total = prefix_k.shape[0]
    pblock = min(512, prefix_total)
    prefix_allowed = jnp.broadcast_to(live_rows[:, None], (token_rows, pblock))

    def split_heads(slot_table):
        return slot_table.reshape(slot_table.shape[0], KEY_HEADS, HEAD_SIZE)

    def scores(key_rows):
        return scale * jnp.einsum(
            "tkgd,nkd->kgtn",
            query_head_split,
            split_heads(key_rows),
            preferred_element_type=jnp.float32,
        )

    def value_products(value_rows):
        return jnp.einsum(
            "tkgd,nkd->kgtn",
            output_gradient_heads,
            split_heads(value_rows),
            preferred_element_type=jnp.float32,
        )

    def self_allowed(start, width):
        key_seg = lax.dynamic_slice_in_dim(seg_all, start, width)
        key_slot = start + jnp.arange(width, dtype=jnp.int32)
        return (
            (seg_rows[:, None] == key_seg[None, :])
            & (key_slot[None, :] <= my_slots[:, None])
            & live_rows[:, None]
        )

    def stats_step(carry, key_rows, value_rows, allowed):
        top, total, weighted = carry
        score = jnp.where(allowed[None, None], scores(key_rows), NEG)
        new_top = jnp.maximum(top, jnp.max(score, axis=-1))
        prob = jnp.where(allowed[None, None], jnp.exp(score - new_top[..., None]), 0.0)
        factor = jnp.exp(top - new_top)
        dprob = value_products(value_rows)
        return (
            new_top,
            total * factor + jnp.sum(prob, axis=-1),
            weighted * factor + jnp.sum(prob * dprob, axis=-1),
        )

    first_live = live_rows[0]
    start_first = jnp.sum(jnp.where(seg_rows[0] == jnp.arange(starts.shape[0]), starts, 0))
    low_slot = jnp.where(first_live, start_first, first_slot)
    low_block = low_slot // block
    high_block = jnp.where(first_live, (first_slot + token_rows + block - 1) // block, low_block)
    statistics_shape = (KEY_HEADS, GROUP_QUERIES, token_rows)
    carry = (
        jnp.full(statistics_shape, NEG, jnp.float32),
        jnp.zeros(statistics_shape, jnp.float32),
        jnp.zeros(statistics_shape, jnp.float32),
    )

    def prefix_stats(number, carry):
        start = number * pblock
        key_rows = lax.dynamic_slice_in_dim(prefix_k, start, pblock)
        value_rows = lax.dynamic_slice_in_dim(prefix_v, start, pblock)
        return stats_step(carry, key_rows, value_rows, prefix_allowed)

    carry = lax.fori_loop(0, prefix_total // pblock, prefix_stats, carry)

    def stats_block(number, carry):
        start = number * block
        key_rows = lax.dynamic_slice_in_dim(resp_k, start, block)
        value_rows = lax.dynamic_slice_in_dim(resp_v, start, block)
        return stats_step(carry, key_rows, value_rows, self_allowed(start, block))

    top, total, weighted = lax.fori_loop(low_block, high_block, stats_block, carry)
    live_stats = live_rows[None, None, :]
    total_safe = jnp.where(live_stats, total, 1.0)
    log_total = jnp.where(live_stats, top + jnp.log(total_safe), 0.0)
    delta = weighted / total_safe

    def grad_terms(key_rows, value_rows, allowed):
        prob = jnp.where(allowed[None, None], jnp.exp(scores(key_rows) - log_total[..., None]), 0.0)
        dprob = value_products(value_rows)
        dscore = prob * (dprob - delta[..., None])
        prob_b = prob.astype(jnp.bfloat16)
        dscore_b = dscore.astype(jnp.bfloat16)
        dq_term = scale * jnp.einsum(
            "kgtn,nkd->tkgd", dscore_b, split_heads(key_rows), preferred_element_type=jnp.float32
        )
        dk_term = scale * jnp.einsum(
            "kgtn,tkgd->nkd", dscore_b, query_head_split, preferred_element_type=jnp.float32
        )
        dv_term = jnp.einsum(
            "kgtn,tkgd->nkd", prob_b, output_gradient_heads, preferred_element_type=jnp.float32
        )
        return (dq_term, dk_term.reshape(-1, kv_width), dv_term.reshape(-1, kv_width))

    query_gradient_blank = jnp.zeros((token_rows, KEY_HEADS, GROUP_QUERIES, HEAD_SIZE), jnp.float32)
    prefix_empty = jnp.zeros((prefix_total, kv_width), jnp.float32)

    def prefix_grad(number, carry):
        dq_acc, dk_acc, dv_acc = carry
        start = number * pblock
        key_rows = lax.dynamic_slice_in_dim(prefix_k, start, pblock)
        value_rows = lax.dynamic_slice_in_dim(prefix_v, start, pblock)
        dq_term, dk_term, dv_term = grad_terms(key_rows, value_rows, prefix_allowed)
        dk_acc = lax.dynamic_update_slice_in_dim(dk_acc, dk_term, start, 0)
        dv_acc = lax.dynamic_update_slice_in_dim(dv_acc, dv_term, start, 0)
        return (dq_acc + dq_term, dk_acc, dv_acc)

    dq_prefix, dk_prefix, dv_prefix = lax.fori_loop(
        0, prefix_total // pblock, prefix_grad, (query_gradient_blank, prefix_empty, prefix_empty)
    )
    empty_keys = jnp.zeros((total_slots, kv_width), jnp.float32)

    def grad_block(number, carry):
        dq_acc, dk_acc, dv_acc = carry
        start = number * block
        key_rows = lax.dynamic_slice_in_dim(resp_k, start, block)
        value_rows = lax.dynamic_slice_in_dim(resp_v, start, block)
        dq_term, dk_term, dv_term = grad_terms(key_rows, value_rows, self_allowed(start, block))
        dk_acc = lax.dynamic_update_slice_in_dim(
            dk_acc, lax.dynamic_slice_in_dim(dk_acc, start, block) + dk_term, start, 0
        )
        dv_acc = lax.dynamic_update_slice_in_dim(
            dv_acc, lax.dynamic_slice_in_dim(dv_acc, start, block) + dv_term, start, 0
        )
        return (dq_acc + dq_term, dk_acc, dv_acc)

    dq_total, dk_self, dv_self = lax.fori_loop(
        low_block, high_block, grad_block, (dq_prefix, empty_keys, empty_keys)
    )
    dk_resp, dv_resp, dk_part, dv_part = (
        lax.psum_scatter(dk_self, "ctx", scatter_dimension=0, tiled=True),
        lax.psum_scatter(dv_self, "ctx", scatter_dimension=0, tiled=True),
        lax.psum_scatter(dk_prefix, "ctx", scatter_dimension=0, tiled=True),
        lax.psum_scatter(dv_prefix, "ctx", scatter_dimension=0, tiled=True),
    )
    prefix_key_gradient, prefix_value_gradient = sum_prefix_totals(dk_part, dv_part)
    grad_q = dq_total.reshape(1, token_rows, QUERY_HEADS * HEAD_SIZE).astype(jnp.bfloat16)
    grad_kr = dk_resp.astype(jnp.bfloat16).reshape(1, token_rows, kv_width)
    grad_vr = dv_resp.astype(jnp.bfloat16).reshape(1, token_rows, kv_width)
    return (grad_q, prefix_key_gradient, prefix_value_gradient, grad_kr, grad_vr)


def solution(mesh):
    in_specs = (
        P(("dp", "smp"), "ctx", None),
        P(("dp", "ctx"), None),
        P(("dp", "ctx"), None),
        P(("dp", "smp"), "ctx", None),
        P(("dp", "smp"), "ctx", None),
        P(("dp", "smp"), "ctx", None),
        P("dp"),
        P("dp"),
    )
    out_specs = (
        P(("dp", "smp"), "ctx", None),
        P(("dp", "ctx"), None),
        P(("dp", "ctx"), None),
        P(("dp", "smp"), "ctx", None),
        P(("dp", "smp"), "ctx", None),
    )
    return jax.shard_map(shards, mesh=mesh, in_specs=in_specs, out_specs=out_specs, check_vma=False)
```

profile of v0, /device:TPU:1, one launch (start us, length us, event | category | flops | bytes accessed | tf_op | source)
XLA Modules:
  0.0 706.4 jit_solution(1648139505316569918)
XLA Ops:
  8.7 1.7 copy.132
  10.4 1.7 copy.133
  16.1 1.6 copy.126
  18.4 2.3 copy.127
  20.7 1.6 copy.131
  22.3 44.3 %all-gather.7.cloned.1.call-done = bf16[1024,512]{1,0:T(8,128)(2,1)} async-done(((bf16[64,512]{1,0:T(8,128)(2,1)}), bf16[1024,512]{1,0:T(8,128)(2,1)}) %all-gather.7.cloned.1.call-update) | async-done | bytes 1048592 | tf_op jit(solution)/shard_map/all_gather | solution.py:59
  66.6 2.3 copy.136
  68.9 51.0 %all-gather.9.cloned.1.call-done = bf16[1024,512]{1,0:T(8,128)(2,1)} async-done(((bf16[64,512]{1,0:T(8,128)(2,1)}), bf16[1024,512]{1,0:T(8,128)(2,1)}) %all-gather.9.cloned.1.call-update) | async-done | bytes 1048592 | tf_op jit(solution)/shard_map/all_gather | solution.py:60
  119.9 2.3 copy.130
  122.1 15.2 %while.68 = (s32[]{:T(128)}, f32[4,8,128]{2,1,0:T(8,128)S(1)}, f32[4,8,128]{2,1,0:T(8,128)S(1)}, f32[4,8,128]{2,1,0:T(8,128)S(1)}, bf16[1024,512]{0,1:T(8,128)(2...) while((s32[]{:T(128)}, f32[4,8,128]{2,1,0:T(8,128)S(1)}, ...), condition=%wide.region_7.8_spmd.clone, body=%wide.region_3.7_spmd.clone.sunk | while | flops 1103130624 | bytes 30704192 | solution.py:133
  123.4 1.4 fusion.140
  124.8 2.9 fusion.141
  127.7 2.0 fusion.142
  131.0 1.4 fusion.140
  132.5 2.9 fusion.141
  135.4 2.0 fusion.142
  137.4 46.6 %all-gather.11.cloned.1.call-done = bf16[1,2048,512]{1,2,0:T(8,128)(2,1)} async-done(((bf16[1,128,512]{1,2,0:T(8,128)(2,1)}), bf16[1,2048,512]{1,2,0:T(8,128)(2,1)}) %all-gather.11.cloned.1.call-update) | async-done | bytes 2097168 | tf_op jit(solution)/shard_map/all_gather | solution.py:63
  184.0 63.2 %all-gather.13.cloned.1.call-done = bf16[1,2048,512]{1,2,0:T(8,128)(2,1)} async-done(((bf16[1,128,512]{1,2,0:T(8,128)(2,1)}), bf16[1,2048,512]{1,2,0:T(8,128)(2,1)}) %all-gather.13.cloned.1.call-update) | async-done | bytes 2097168 | tf_op jit(solution)/shard_map/all_gather | solution.py:64
  247.2 8.4 %while.66 = (s32[]{:T(128)}, f32[4,8,128]{2,1,0:T(8,128)S(1)}, f32[4,8,128]{2,1,0:T(8,128)S(1)}, f32[4,8,128]{2,1,0:T(8,128)S(1)}, s32[]{:T(128)}, /*index=5*/s3...) while((s32[]{:T(128)}, f32[4,8,128]{2,1,0:T(8,128)S(1)}, ...), condition=%wide.region_12.13_spmd.clone, body=%wide.region_8.12_spmd.clone.sunk | while | flops 1103377024 | bytes 30977884 | solution.py:141
  247.5 1.3 constant_dynamic-slice_fusion.18
  248.8 1.5 fusion.119
  250.3 3.0 fusion.120
  253.3 2.1 fusion.121
  255.6 1.6 broadcast_in_dim.156.clone2
  257.2 1.6 broadcast_in_dim.156.clone
  258.8 57.3 %while.69 = (s32[]{:T(128)}, f32[128,4,8,128]{0,3,2,1:T(8,128)}, f32[1024,512]{1,0:T(8,128)}, f32[1024,512]{1,0:T(8,128)}, bf16[1024,512]{0,1:T(8,128)(2,1)}, /*...) while((s32[]{:T(128)}, f32[128,4,8,128]{0,3,2,1:T(8,128)}, ...), condition=%wide.region_14.15_spmd.clone, body=%wide.region_13.14_spmd.clone.sunk | while | flops 2707161088 | bytes 98091616 | solution.py:177
  261.8 1.3 fusion.154
  263.1 3.9 fusion.156
  267.0 5.5 fusion.155
  272.5 2.7 copy.204
  275.2 4.8 fusion.157
  281.1 3.3 copy.205
  284.4 3.1 constant_dynamic-update-slice_fusion.7
  290.4 1.3 fusion.154
  291.7 3.9 fusion.156
  295.6 5.5 fusion.155
  301.1 2.7 copy.204
  303.8 4.8 fusion.157
  309.7 3.3 copy.205
  313.0 3.1 constant_dynamic-update-slice_fusion.7
  316.8 2.5 broadcast_in_dim.161.clone2
  319.3 2.5 broadcast_in_dim.161.clone
  321.8 40.5 %while.67 = (s32[]{:T(128)}, f32[128,4,8,128]{0,3,2,1:T(8,128)S(1)}, f32[2048,512]{1,0:T(8,128)}, f32[2048,512]{1,0:T(8,128)}, s32[]{:T(128)}, /*index=5*/bf16[2...) while((s32[]{:T(128)}, ...), condition=%wide.region_16.17_spmd.clone, body=%wide.region_15.16_spmd.clone.sunk | while | flops 2707423744 | bytes 104591360 | solution.py:196
  322.1 1.9 constant_dynamic-slice_fusion.20
  324.0 1.8 constant_dynamic-slice_fusion.19
  325.8 2.3 constant_dynamic-slice_fusion.21
  328.1 2.6 copy.200
  330.6 2.3 constant_dynamic-slice_fusion.22
  332.9 2.6 copy.202
  335.5 2.3 fusion.132
  337.8 3.1 fusion.134
  341.0 5.6 fusion.133
  347.8 2.6 copy.201
  350.4 3.9 fusion.135
  356.6 2.6 copy.203
  359.2 3.0 constant_dynamic-update-slice_fusion.6
  363.2 1.3 copy.167
  364.5 49.1 %reduce-scatter.7.cloned.1.call-done = f32[64,512]{1,0:T(8,128)} async-done(((f32[1024,512]{1,0:T(8,128)}), f32[64,512]{1,0:T(8,128)}) %reduce-scatter.7.cloned.1.call-update) | async-done | bytes 131088 | tf_op jit(solution)/shard_map/reduce_scatter | solution.py:203
  413.6 89.7 %reduce-scatter.5.cloned.1.call-done = f32[64,512]{1,0:T(8,128)} async-done(((f32[1024,512]{1,0:T(8,128)}), f32[64,512]{1,0:T(8,128)}) %reduce-scatter.5.cloned.1.call-update) | async-done | bytes 131088 | tf_op jit(solution)/shard_map/reduce_scatter | solution.py:202
  503.3 27.3 %all-reduce.2 = (bf16[64,512]{1,0:T(8,128)(2,1)}, bf16[64,512]{1,0:T(8,128)(2,1)}) all-reduce(f32[64,512]{1,0:T(8,128)} %reduce-scatter.5.cloned.1.call-done, f32[64,512]{1,0:T(8,128)} %reduce-scatter.7.cloned.1.call-done), channel_id=1, replica_groups=mesh['ctx'=16,'smp'=8,'dp'=2] {'smp'}, use_global_device_ids=true, to_apply=%region_18.19 | all-reduce | flops 65536 | bytes 393216 | tf_op jit(solution)/shard_map/psum | solution.py:32
  530.6 70.3 %reduce-scatter.11.cloned.1.call-done = f32[128,512]{1,0:T(8,128)} async-done(((f32[2048,512]{1,0:T(8,128)}), f32[128,512]{1,0:T(8,128)}) %reduce-scatter.11.cloned.1.call-update) | async-done | bytes 262160 | tf_op jit(solution)/shard_map/reduce_scatter | solution.py:201
  600.9 1.6 convert_bitcast_fusion
  602.6 95.3 %reduce-scatter.9.cloned.1.call-done = f32[128,512]{1,0:T(8,128)} async-done(((f32[2048,512]{1,0:T(8,128)}), f32[128,512]{1,0:T(8,128)}) %reduce-scatter.9.cloned.1.call-update) | async-done | bytes 262160 | tf_op jit(solution)/shard_map/reduce_scatter | solution.py:200
  697.9 1.6 convert_bitcast_fusion.1
  (93 shorter events, 21.8 us)
Async XLA Ops:
  7.2 59.5 %all-gather.7.cloned.1.call-start = ((), (), s32[]{:S(2)}) async-start(), calls=%async_computation.4 | async-start | bytes 1114112 | tf_op jit(solution)/shard_map/all_gather | solution.py:59
  7.9 112.0 %all-gather.9.cloned.1.call-start = ((), (), s32[]{:S(2)}) async-start(), calls=%async_computation.5 | async-start | bytes 1114112 | tf_op jit(solution)/shard_map/all_gather | solution.py:60
  8.6 175.4 %all-gather.11.cloned.1.call-start = ((), (), s32[]{:S(2)}) async-start(), calls=%async_computation.10 | async-start | bytes 2228224 | tf_op jit(solution)/shard_map/all_gather | solution.py:63
  10.4 236.8 %all-gather.13.cloned.1.call-start = ((), (), s32[]{:S(2)}) async-start(), calls=%async_computation.11 | async-start | bytes 2228224 | tf_op jit(solution)/shard_map/all_gather | solution.py:64
  12.1 401.5 %reduce-scatter.7.cloned.1.call-start = ((), (), s32[]{:S(2)}) async-start(), calls=%async_computation.7 | async-start | bytes 2228224 | tf_op jit(solution)/shard_map/reduce_scatter | solution.py:203
  261.0 0.8 copy-start.6
  272.4 7.5 %copy-start.2 = (f32[128,4,8,128]{0,3,2,1:T(8,128)S(1)}, f32[128,4,8,128]{0,3,2,1:T(8,128)}, u32[]{:S(2)}) copy-start(f32[128,4,8,128]{0,3,2,1:T(8,128)} %get-tuple-element.1307) | copy-start | bytes 6291460 | tf_op jit(solution)/shard_map/while
  275.2 4.8 copy-start.1
  275.2 4.8 copy-start.7
  281.1 6.4 copy-start.3
  289.6 0.8 copy-start.6
  301.1 7.5 %copy-start.2 = (f32[128,4,8,128]{0,3,2,1:T(8,128)S(1)}, f32[128,4,8,128]{0,3,2,1:T(8,128)}, u32[]{:S(2)}) copy-start(f32[128,4,8,128]{0,3,2,1:T(8,128)} %get-tuple-element.1307) | copy-start | bytes 6291460 | tf_op jit(solution)/shard_map/while
  303.8 4.8 copy-start.1
  303.8 4.8 copy-start.7
  309.7 6.4 copy-start.3
  316.1 5.6 copy-start.4
  316.1 187.1 %reduce-scatter.5.cloned.1.call-start = ((), (), s32[]{:S(2)}) async-start(), calls=%async_computation.6 | async-start | bytes 2228224 | tf_op jit(solution)/shard_map/reduce_scatter | solution.py:202
  316.7 284.2 %reduce-scatter.11.cloned.1.call-start = ((), (), s32[]{:S(2)}) async-start(), calls=%async_computation.9 | async-start | bytes 4456448 | tf_op jit(solution)/shard_map/reduce_scatter | solution.py:201
  337.8 3.1 copy-start.10
  340.9 5.6 copy-start.9
  350.4 3.9 copy-start
  350.4 3.9 copy-start.5
  350.4 5.0 copy-start.8
  362.2 335.7 %reduce-scatter.9.cloned.1.call-start = ((), (), s32[]{:S(2)}) async-start(), calls=%async_computation.8 | async-start | bytes 4456448 | tf_op jit(solution)/shard_map/reduce_scatter | solution.py:200
Sparse Core Ops, SparseCore 0:
  10.4 56.1 all-gather.6
  69.0 50.7 all-gather.8
  122.8 61.1 all-gather.10
  186.8 60.3 all-gather.12
  316.3 97.2 reduce-scatter.6
  417.4 85.8 reduce-scatter.4
  506.9 93.9 reduce-scatter.10
  605.0 92.8 reduce-scatter.8
where the time goes:
time: 709 us; the launch traced here: 706 us
  waiting for transfers between devices  512 us (72%)
  local copies, waits for them, and re-layouts  73.3 us (10%)
  matrix products  62.2 us (9%)
  blocking collectives  27.3 us (4%)
  other arithmetic  15.4 us (2%)
  between operations  15 us (2%)
    reduce_scatter x1, waiting for transfers between devices, shards(): lax.psum_scatter(dk_self, 'ctx', scatter_dimension=0, tiled=True)  95.3 us
    reduce_scatter x1, waiting for transfers between devices, shards(): lax.psum_scatter(dk_prefix, 'ctx', scatter_dimension=0, tiled=True)  89.7 us
    reduce_scatter x1, waiting for transfers between devices, shards(): lax.psum_scatter(dv_self, 'ctx', scatter_dimension=0, tiled=True)  70.3 us
    all_gather x1, waiting for transfers between devices, shards(): lax.all_gather(value_response[0], 'ctx', axis=0, tiled=True)  63.2 us
    all_gather x1, waiting for transfers between devices, shards(): lax.all_gather(value_prefix, 'ctx', axis=0, tiled=True)  51 us
    reduce_scatter x1, waiting for transfers between devices, shards(): lax.psum_scatter(dv_prefix, 'ctx', scatter_dimension=0, tiled=True)  49.1 us
    all_gather x1, waiting for transfers between devices, shards(): lax.all_gather(key_response[0], 'ctx', axis=0, tiled=True)  46.6 us
    all_gather x1, waiting for transfers between devices, shards(): lax.all_gather(key_prefix, 'ctx', axis=0, tiled=True)  44.3 us
  transfers between devices with their start and end apart: 8, of which 8 were waited for; matrix products, arithmetic and copies ran while one was open for 11% of the time, Pallas kernels for 0%

commit v1 on v0

v1 whole, which is shorter than its diff:
```python
import functools

import jax
import jax.numpy as jnp
from jax import lax
from jax.experimental import pallas as pl
from jax.experimental.pallas import tpu as pltpu
from jax.sharding import PartitionSpec as P

HEADS = 4
GROUP = 8
DIM = 128
ROWS = 128
PREFIX = 1024
WINDOW = 9 * ROWS
KEYS = PREFIX + WINDOW
QB = 256
STEPS = GROUP * ROWS // QB
SIDE = 4
SCALE = DIM ** -0.5
LOG2E = 1.4426950408889634
MASKED = -1e30
RESPONSES = 16
MESH = pl.DeviceIdType.MESH


def dot_nt(a, b):
    return lax.dot_general(a, b, (((1,), (1,)), ((), ())), preferred_element_type=jnp.float32)


def dot_nn(a, b):
    return lax.dot_general(a, b, (((1,), (0,)), ((), ())), preferred_element_type=jnp.float32)


def fold(x, op):
    return op(x.reshape(x.shape[0] // 8, 8, x.shape[1]), axis=0)


def attend(h, qb, q_v, do_v, pre, win, bias, live, s_scr, dp_scr, acc, kt, dq_v):
    col = pl.multiple_of(h * (GROUP * DIM) + qb * QB, QB)
    qa = q_v[:, pl.ds(col, QB)]
    da = do_v[:, pl.ds(col, QB)]
    qs = jnp.concatenate([qa[:, :DIM], qa[:, DIM:]], axis=0)
    ds_ = jnp.concatenate([da[:, :DIM], da[:, DIM:]], axis=0)
    chunks = [(256 * i, 256) for i in range(4)] + [(PREFIX + 384 * i, 384) for i in range(3)]

    def rows_of(kv, start, size):
        if start < PREFIX:
            return pre[h, kv, pl.ds(start, size), :]
        return win[h, kv, pl.ds((start - PREFIX) // ROWS, size // ROWS)].reshape(size, DIM)

    top8 = jnp.full((8, QB), MASKED, jnp.float32)
    for start, size in chunks:
        s = dot_nt(rows_of(0, start, size), qs)
        if start >= PREFIX:
            b = bias[pl.ds(start - PREFIX, size), :]
            s = s + jnp.concatenate([b, b], axis=1)
        s_scr[pl.ds(start, size), :] = s
        top8 = jnp.maximum(top8, fold(s, jnp.max))
    factor = SCALE * LOG2E
    shift = jnp.max(top8, axis=0, keepdims=True) * factor
    sum8 = jnp.zeros((8, QB), jnp.float32)
    dot8 = jnp.zeros((8, QB), jnp.float32)
    for start, size in chunks:
        p = jnp.exp2(s_scr[pl.ds(start, size), :] * factor - shift)
        dp = dot_nt(rows_of(1, start, size), ds_)
        s_scr[pl.ds(start, size), :] = p
        dp_scr[pl.ds(start, size), :] = dp
        sum8 = sum8 + fold(p, jnp.sum)
        dot8 = dot8 + fold(p * dp, jnp.sum)
    inverse = 1.0 / jnp.sum(sum8, axis=0, keepdims=True)
    delta = jnp.sum(dot8, axis=0, keepdims=True) * inverse
    live_row = live[...]
    inverse = inverse * jnp.concatenate([live_row, live_row], axis=1)
    dqt = jnp.zeros((DIM, QB), jnp.float32)
    for start, size in chunks:
        p = s_scr[pl.ds(start, size), :] * inverse
        dsc = (p * (dp_scr[pl.ds(start, size), :] - delta)).astype(jnp.bfloat16)
        pb = p.astype(jnp.bfloat16)
        acc[h, 1, pl.ds(start, size), :] += dot_nn(pb, ds_)
        acc[h, 0, pl.ds(start, size), :] += dot_nn(dsc, qs)
        dqt = dqt + dot_nn(kt[:, pl.ds(start, size)], dsc)
    dq = (dqt * SCALE).T.astype(jnp.bfloat16)
    dq_v[:, pl.ds(col, QB)] = jnp.concatenate([dq[:ROWS], dq[ROWS:]], axis=1)


def transpose_keys(h, pre, win, kt):
    for i in range(4):
        kt[:, pl.ds(256 * i, 256)] = pre[h, 0, pl.ds(256 * i, 256), :].T
    for i in range(9):
        kt[:, pl.ds(PREFIX + ROWS * i, ROWS)] = win[h, 0, i].T


def masks(place, smp, len_ref, asg_ref, bias, live):
    slot = place * ROWS + lax.broadcasted_iota(jnp.int32, (1, ROWS), 1)
    first = jnp.full((1, ROWS), 1 << 20, jnp.int32)
    start = jnp.int32(0)
    for r in range(RESPONSES):
        stop = start + jnp.where(asg_ref[r] == smp, len_ref[r], 0)
        first = jnp.where((slot >= start) & (slot < stop), start, first)
        start = stop
    live[...] = jnp.where(first < (1 << 20), 1.0, 0.0).astype(jnp.float32)
    for i in range(9):
        key = (place - 8 + i) * ROWS + lax.broadcasted_iota(jnp.int32, (ROWS, ROWS), 0)
        allowed = (key >= first) & (key <= slot)
        bias[pl.ds(i * ROWS, ROWS), :] = jnp.where(allowed, 0.0, MASKED).astype(jnp.float32)


def kernel(
    q_hbm, kp_hbm, vp_hbm, kr_hbm, vr_hbm, do_hbm, len_ref, asg_ref,
    dq_hbm, dkp_hbm, dvp_hbm, dkr_hbm, dvr_hbm,
    q_v, do_v, dq_v, pre, win, bias, live, s_scr, dp_scr, acc, kt,
    rsend, rrecv, zsend, zrecv,
    csend, crecv, xsend, xrecv, ysend, yrecv, wsend, wrecv, finall,
    okr, okp,
    local, gz_s, gz_r, gy_s, gy_r, pz_s, pz_r, py_s, py_r, px_s, px_r, pc_s, pc_r,
    ry_s, ry_r, rz_s, rz_r, rc_s, rc_r, rx_s, rx_r, rp_s, rp_r, rw_s, rw_r, rf_s, rf_r,
):
    ctx = lax.axis_index("ctx")
    smp = lax.axis_index("smp")
    z, y = ctx // SIDE, ctx % SIDE
    x, core = smp // 2, smp % 2
    other = 1 - core

    def at_z(o):
        return {"ctx": ((z + o) % SIDE) * SIDE + y}

    def at_y(o):
        return {"ctx": z * SIDE + (y + o) % SIDE}

    def at_x(o):
        return {"smp": ((x + o) % SIDE) * 2 + core}

    at_core = {"smp": x * 2 + other}

    def send(src, dst, ss, rs, where):
        return pltpu.make_async_remote_copy(
            src_ref=src, dst_ref=dst, send_sem=ss, recv_sem=rs, device_id=where, device_id_type=MESH
        )

    loads = []
    for h in range(HEADS):
        cols = pl.ds(h * DIM, DIM)
        loads.append(pltpu.make_async_copy(kr_hbm.at[0, :, cols], win.at[h, 0, 8], local.at[2 * h]))
        loads.append(pltpu.make_async_copy(vr_hbm.at[0, :, cols], win.at[h, 1, 8], local.at[2 * h + 1]))
    mine = pl.ds(pl.multiple_of(x * 256 + y * 64 + z * 16, 16), 16)
    from_rows = pl.ds(pl.multiple_of(x * 16, 16), 16)

    def load_prefix(h, src):
        return pltpu.make_async_copy(
            src.at[from_rows, pl.ds(h * DIM, DIM)], pre.at[h, core, mine, :], local.at[8 + h]
        )

    for copy in loads:
        copy.start()

    @pl.when(core == 0)
    def _():
        for h in range(HEADS):
            load_prefix(h, kp_hbm).start()

    @pl.when(core == 1)
    def _():
        for h in range(HEADS):
            load_prefix(h, vp_hbm).start()

    load_q = pltpu.make_async_copy(q_hbm.at[0], q_v, local.at[12])
    load_do = pltpu.make_async_copy(do_hbm.at[0], do_v, local.at[13])
    load_q.start()
    load_do.start()

    barrier = pltpu.get_barrier_semaphore()
    partners = [at_z(o) for o in (1, 2, 3)] + [at_y(o) for o in (1, 2, 3)]
    smp_partners = [{"smp": (smp + o) % 8} for o in range(1, 8)]
    for where in partners + smp_partners:
        pl.semaphore_signal(barrier, inc=1, device_id=where, device_id_type=MESH)
    for copy in loads:
        copy.wait()
    for h in range(HEADS):
        load_prefix(h, kp_hbm).wait()
    pl.semaphore_wait(barrier, len(partners) + len(smp_partners))

    def gather_z(h, step):
        src, dst = (8, 4) if step == 0 else (4, 0)
        return send(win.at[h, :, src], win.at[h, :, dst], gz_s.at[h, step], gz_r.at[h, step], at_z(1))

    def gather_y(h, o, part):
        d = jnp.where(y + o < SIDE, o, o - SIDE)
        if part == 0:
            src, dst = 4, 4 - d
        else:
            src, dst = jnp.where(d > 0, 8, 0), jnp.where(d > 0, 8 - d, -d)
        return send(win.at[h, :, src], win.at[h, :, dst], gy_s.at[h, o - 1, part], gy_r.at[h, o - 1, part], at_y(o))

    def gather_a(h):
        gather_z(h, 0).start()

    def gather_b(h):
        gather_z(h, 0).wait_recv()
        gather_z(h, 1).start()
        for o in (1, 2, 3):
            gather_y(h, o, 0).start()

    def gather_c(h):
        gather_z(h, 1).wait_recv()
        for o in (1, 2, 3):
            gather_y(h, o, 1).start()

    def gather_d(h):
        for o in (1, 2, 3):
            gather_y(h, o, 0).wait_recv()
            gather_y(h, o, 1).wait_recv()

    def prefix_z(o):
        return send(pre.at[:, core, mine, :], pre.at[:, core, mine, :], pz_s.at[o - 1], pz_r.at[o - 1], at_z(o))

    def prefix_y(o):
        rows = pl.ds(pl.multiple_of(x * 256 + y * 64, 64), 64)
        return send(pre.at[:, core, rows, :], pre.at[:, core, rows, :], py_s.at[o - 1], py_r.at[o - 1], at_y(o))

    def prefix_x(h, o):
        rows = pl.ds(pl.multiple_of(x * 256, 256), 256)
        return send(
            pre.at[h, core, rows, :], pre.at[h, core, rows, :], px_s.at[h, o - 1], px_r.at[h, o - 1], at_x(o)
        )

    def prefix_c(h):
        return send(pre.at[h, core], pre.at[h, core], pc_s.at[h], pc_r.at[h], at_core)

    def prefix_last(h):
        for o in (1, 2, 3):
            prefix_x(h, o).wait_recv()
        prefix_c(h).start()

    def reduce_y(h, o, part):
        d = jnp.where(y + o < SIDE, o, o - SIDE)
        src = 4 + d if part == 0 else jnp.where(d > 0, d, 8 + d)
        return send(
            rsend.at[h, src], rrecv.at[h, o - 1, part], ry_s.at[h, o - 1, part], ry_r.at[h, o - 1, part], at_y(o)
        )

    def reduce_z(h, step):
        return send(zsend.at[h, step], zrecv.at[h, step], rz_s.at[h, step], rz_r.at[h, step], at_z(3))

    def slot_rows(i):
        return pl.ds(PREFIX + i * ROWS, ROWS)

    def reduce_a(h):
        for i in range(9):
            for kv in range(2):
                rsend[h, i, kv] = acc[h, kv, slot_rows(i), :].astype(jnp.bfloat16)
        for o in (1, 2, 3):
            for part in (1, 0):
                reduce_y(h, o, part).start()

    def reduce_b(h):
        for o in (1, 2, 3):
            reduce_y(h, o, 0).wait_recv()
            reduce_y(h, o, 1).wait_recv()
        for kv in range(2):
            far = acc[h, kv, slot_rows(0), :]
            mid = acc[h, kv, slot_rows(4), :]
            near = acc[h, kv, slot_rows(8), :]
            for o in (1, 2, 3):
                mid = mid + rrecv[h, o - 1, 0, kv].astype(jnp.float32)
                term = rrecv[h, o - 1, 1, kv].astype(jnp.float32)
                lower = jnp.where(y >= o, 1.0, 0.0).astype(jnp.float32)
                far = far + term * lower
                near = near + term * (1.0 - lower)
            zsend[h, 0, kv] = far.astype(jnp.bfloat16)
            acc[h, kv, slot_rows(4), :] = mid
            acc[h, kv, slot_rows(8), :] = near
        reduce_z(h, 0).start()

    def reduce_c(h):
        reduce_z(h, 0).wait_recv()
        for kv in range(2):
            mid = acc[h, kv, slot_rows(4), :] + zrecv[h, 0, kv].astype(jnp.float32)
            zsend[h, 1, kv] = mid.astype(jnp.bfloat16)
        reduce_z(h, 1).start()

    def reduce_d(h):
        reduce_z(h, 1).wait_recv()
        for kv in range(2):
            near = acc[h, kv, slot_rows(8), :] + zrecv[h, 1, kv].astype(jnp.float32)
            if kv == 0:
                near = near * SCALE
            okr[kv, h] = near.astype(jnp.bfloat16)

    def total_c(h):
        return send(csend.at[h], crecv.at[h], rc_s.at[h], rc_r.at[h], at_core)

    def total_x(h, o):
        return send(
            xsend.at[h, (x + o) % SIDE], xrecv.at[h, o - 1], rx_s.at[h, o - 1], rx_r.at[h, o - 1], at_x(o)
        )

    def total_y(h, o):
        return send(
            ysend.at[h, (y + o) % SIDE], yrecv.at[h, o - 1], rp_s.at[h, o - 1], rp_r.at[h, o - 1], at_y(o)
        )

    def total_z(h, o):
        return send(
            wsend.at[h, (z + o) % SIDE], wrecv.at[h, o - 1], rw_s.at[h, o - 1], rw_r.at[h, o - 1], at_z(o)
        )

    def total_a(h):
        csend[h] = acc[h, other, pl.ds(0, PREFIX), :].astype(jnp.bfloat16)
        total_c(h).start()

    def total_b(h):
        total_c(h).wait_recv()
        for i in range(SIDE):
            rows = pl.ds(256 * i, 256)
            both = acc[h, core, rows, :] + crecv[h, rows, :].astype(jnp.float32)
            acc[h, core, rows, :] = both
            xsend[h, i] = both.astype(jnp.bfloat16)
        for o in (1, 2, 3):
            total_x(h, o).start()

    def total_d(h):
        for o in (1, 2, 3):
            total_x(h, o).wait_recv()
        whole = acc[h, core, pl.ds(pl.multiple_of(x * 256, 256), 256), :]
        for o in (1, 2, 3):
            whole = whole + xrecv[h, o - 1].astype(jnp.float32)
        ysend[h] = whole.reshape(SIDE, 64, DIM)
        for o in (1, 2, 3):
            total_y(h, o).start()

    def total_e(h):
        for o in (1, 2, 3):
            total_y(h, o).wait_recv()
        whole = ysend[h, y]
        for o in (1, 2, 3):
            whole = whole + yrecv[h, o - 1]
        wsend[h] = whole.reshape(SIDE, 16, DIM)
        for o in (1, 2, 3):
            total_z(h, o).start()

    def total_f(h):
        for o in (1, 2, 3):
            total_z(h, o).wait_recv()
        whole = wsend[h, z]
        for o in (1, 2, 3):
            whole = whole + wrecv[h, o - 1]
        whole = whole * jnp.where(core == 0, SCALE, 1.0).astype(jnp.float32)
        finall[smp, h] = whole.astype(jnp.bfloat16)

    def total_g(o):
        return send(finall.at[smp], finall.at[smp], rf_s.at[o - 1], rf_r.at[o - 1], smp_partners[o - 1])

    for o in (1, 2, 3):
        prefix_z(o).start()
    gather_a(0)
    masks(ctx, smp, len_ref, asg_ref, bias, live)
    for o in (1, 2, 3):
        prefix_z(o).wait_recv()
    for o in (1, 2, 3):
        prefix_y(o).start()
    gather_b(0)
    gather_a(1)
    acc[...] = jnp.zeros_like(acc)
    for o in (1, 2, 3):
        prefix_y(o).wait_recv()
    for h in range(HEADS):
        for o in (1, 2, 3):
            prefix_x(h, o).start()
    load_q.wait()
    load_do.wait()
    gather_c(0)
    prefix_last(0)
    gather_b(1)
    gather_a(2)
    gather_d(0)
    prefix_c(0).wait_recv()

    @pl.loop(0, HEADS * STEPS)
    def _(it):
        h, qb = it // STEPS, it % STEPS

        @pl.when((qb == 0) & (h > 0))
        def _():
            gather_d(h)
            prefix_c(h).wait_recv()

        @pl.when(qb == 0)
        def _():
            transpose_keys(h, pre, win, kt)

        attend(h, qb, q_v, do_v, pre, win, bias, live, s_scr, dp_scr, acc, kt, dq_v)

        @pl.when((qb == 0) & (h > 0))
        def _():
            total_b(h - 1)
            reduce_b(h - 1)

        @pl.when((qb == 0) & (h + 1 < HEADS))
        def _():
            gather_c(h + 1)
            prefix_last(h + 1)

        @pl.when((qb == 1) & (h + 2 < HEADS))
        def _():
            gather_b(h + 2)

        @pl.when((qb == 1) & (h + 3 < HEADS))
        def _():
            gather_a(h + 3)

        @pl.when((qb == 1) & (h > 0))
        def _():
            total_d(h - 1)
            reduce_c(h - 1)

        @pl.when((qb == 2) & (h > 0))
        def _():
            total_e(h - 1)
            reduce_d(h - 1)

        @pl.when((qb == 3) & (h > 0))
        def _():
            total_f(h - 1)

        @pl.when(qb == STEPS - 1)
        def _():
            total_a(h)
            reduce_a(h)

    store_q = pltpu.make_async_copy(dq_v, dq_hbm.at[0], local.at[12])
    store_q.start()
    last = HEADS - 1
    total_b(last)
    reduce_b(last)
    total_d(last)
    reduce_c(last)
    total_e(last)
    total_f(last)
    for o in range(1, 8):
        total_g(o).start()
    reduce_d(last)
    stores = []
    for h in range(HEADS):
        cols = pl.ds(h * DIM, DIM)
        stores.append(pltpu.make_async_copy(okr.at[0, h], dkr_hbm.at[0, :, cols], local.at[2 * h]))
        stores.append(pltpu.make_async_copy(okr.at[1, h], dvr_hbm.at[0, :, cols], local.at[2 * h + 1]))
    for copy in stores:
        copy.start()
    for o in range(1, 8):
        total_g(o).wait_recv()
    for kv in range(2):
        for a in range(SIDE):
            for h in range(HEADS):
                okp[kv, pl.ds(16 * a, 16), pl.ds(h * DIM, DIM)] = finall[2 * a + kv, h]
    tail = [
        pltpu.make_async_copy(okp.at[0], dkp_hbm, local.at[8]),
        pltpu.make_async_copy(okp.at[1], dvp_hbm, local.at[9]),
    ]
    for copy in tail:
        copy.start()

    for o in (1, 2, 3):
        prefix_z(o).wait_send()
        prefix_y(o).wait_send()
    for o in range(1, 8):
        total_g(o).wait_send()

    @pl.loop(0, HEADS)
    def _(h):
        prefix_c(h).wait_send()
        total_c(h).wait_send()
        for step in range(2):
            gather_z(h, step).wait_send()
            reduce_z(h, step).wait_send()
        for o in (1, 2, 3):
            prefix_x(h, o).wait_send()
            total_x(h, o).wait_send()
            total_y(h, o).wait_send()
            total_z(h, o).wait_send()
            for part in range(2):
                gather_y(h, o, part).wait_send()
                reduce_y(h, o, part).wait_send()

    for copy in stores + tail + [store_q]:
        copy.wait()


def shards(q, kp, vp, kr, vr, do, lengths, assign):
    bf, f32 = jnp.bfloat16, jnp.float32
    dma = pltpu.SemaphoreType.DMA
    hbm = pl.BlockSpec(memory_space=pl.ANY)
    smem = pl.BlockSpec(memory_space=pltpu.SMEM)
    H = HEADS
    return pl.pallas_call(
        kernel,
        out_shape=(
            jax.ShapeDtypeStruct(q.shape, bf),
            jax.ShapeDtypeStruct(kp.shape, bf),
            jax.ShapeDtypeStruct(vp.shape, bf),
            jax.ShapeDtypeStruct(kr.shape, bf),
            jax.ShapeDtypeStruct(vr.shape, bf),
        ),
        in_specs=[hbm] * 6 + [smem] * 2,
        out_specs=(hbm,) * 5,
        scratch_shapes=[
            pltpu.VMEM((ROWS, H * GROUP * DIM), bf),
            pltpu.VMEM((ROWS, H * GROUP * DIM), bf),
            pltpu.VMEM((ROWS, H * GROUP * DIM), bf),
            pltpu.VMEM((H, 2, PREFIX, DIM), bf),
            pltpu.VMEM((H, 2, 9, ROWS, DIM), bf),
            pltpu.VMEM((WINDOW, ROWS), f32),
            pltpu.VMEM((1, ROWS), f32),
            pltpu.VMEM((KEYS, QB), f32),
            pltpu.VMEM((KEYS, QB), f32),
            pltpu.VMEM((H, 2, KEYS, DIM), f32),
            pltpu.VMEM((DIM, KEYS), bf),
            pltpu.VMEM((H, 9, 2, ROWS, DIM), bf),
            pltpu.VMEM((H, 3, 2, 2, ROWS, DIM), bf),
            pltpu.VMEM((H, 2, 2, ROWS, DIM), bf),
            pltpu.VMEM((H, 2, 2, ROWS, DIM), bf),
            pltpu.VMEM((H, PREFIX, DIM), bf),
            pltpu.VMEM((H, PREFIX, DIM), bf),
            pltpu.VMEM((H, SIDE, 256, DIM), bf),
            pltpu.VMEM((H, 3, 256, DIM), bf),
            pltpu.VMEM((H, SIDE, 64, DIM), f32),
            pltpu.VMEM((H, 3, 64, DIM), f32),
            pltpu.VMEM((H, SIDE, 16, DIM), f32),
            pltpu.VMEM((H, 3, 16, DIM), f32),
            pltpu.VMEM((8, H, 16, DIM), bf),
            pltpu.VMEM((2, H, ROWS, DIM), bf),
            pltpu.VMEM((2, 64, H * DIM), bf),
            dma((14,)),
            dma((H, 2)), dma((H, 2)), dma((H, 3, 2)), dma((H, 3, 2)),
            dma((3,)), dma((3,)), dma((3,)), dma((3,)),
            dma((H, 3)), dma((H, 3)), dma((H,)), dma((H,)),
            dma((H, 3, 2)), dma((H, 3, 2)), dma((H, 2)), dma((H, 2)),
            dma((H,)), dma((H,)), dma((H, 3)), dma((H, 3)),
            dma((H, 3)), dma((H, 3)), dma((H, 3)), dma((H, 3)),
            dma((7,)), dma((7,)),
        ],
        compiler_params=pltpu.CompilerParams(
            collective_id=0, has_side_effects=True, vmem_limit_bytes=56 * 1024 * 1024
        ),
        name="attention_backward",
    )(q, kp, vp, kr, vr, do, lengths, assign)


def solution(mesh):
    rows = P(("dp", "smp"), "ctx", None)
    prefix = P(("dp", "ctx"), None)
    return jax.shard_map(
        shards,
        mesh=mesh,
        in_specs=(rows, prefix, prefix, rows, rows, rows, P("dp"), P("dp")),
        out_specs=(rows, prefix, prefix, rows, rows),
        check_vma=False,
    )
```

time: 709 us -> 131 us (0.18)
  waiting for transfers between devices: 512 us -> 0 us
  Pallas kernels: 0 us -> 125 us
  local copies, waits for them, and re-layouts: 73.3 us -> 5.2 us
  matrix products: 62.2 us -> 0 us
  blocking collectives: 27.3 us -> 0 us
  other arithmetic: 15.4 us -> 0 us
  between operations: 15 us -> 0.66 us
    reduce_scatter x4 -> x0, waiting for transfers between devices: 304 us -> none  [the longest x1 95.3 us: shards(): lax.psum_scatter(dk_self, 'ctx', scatter_dimension=0, tiled=True)]
    all_gather x4 -> x0, waiting for transfers between devices: 205 us -> none  [the longest x1 63.2 us: shards(): lax.all_gather(value_response[0], 'ctx', axis=0, tiled=True)]
    pallas_call x0 -> x1, Pallas kernels: none -> 125 us  [shards(): pl.pallas_call(kernel, out_shape=(jax.ShapeDtypeStruct(q.shape, bf), jax....]
    dot_general x21 -> x0, matrix products: 62.2 us -> none  [the longest x6 25.3 us: value_products(): jnp.einsum('tkgd,nkd->kgtn', output_gradient_heads, split_heads(value_row...]
    psum x1 -> x0, blocking collectives: 27.3 us -> none  [sum_prefix_totals(): dk_sum, dv_sum = lax.psum((dk_part, dv_part), 'smp')]
    dynamic_update_slice x9 -> x0, local copies, waits for them, and re-layouts: 26.3 us -> none  [the longest x4 11.6 us: prefix_grad(): dv_acc = lax.dynamic_update_slice_in_dim(dv_acc, dv_term, start, 0)]
    dynamic_slice x15 -> x0, local copies, waits for them, and re-layouts: 21.7 us -> none  [the longest x2 4.82 us: grad_block(): lax.dynamic_slice_in_dim(dk_acc, start, block) + dk_term]
    unnamed x10 -> x13, local copies, waits for them, and re-layouts: 14 us -> 5.2 us
  transfers between devices with their start and end apart: 8 -> 0, of which waited for: 8 -> 0; matrix products, arithmetic and copies ran while one was open for 11% -> 0% of each run, Pallas kernels for 0% -> 0%
where the time goes in v1:
time: 131 us
  Pallas kernels  125 us (95%)
  local copies, waits for them, and re-layouts  5.2 us (4%)
    pallas_call x1, Pallas kernels, shards(): pl.pallas_call(kernel, out_shape=(jax.ShapeDtypeStruct(q.shape, bf), jax....  125 us
    unnamed x13, local copies, waits for them, and re-layouts  5.2 us

profile of v1, /device:TPU:1, one launch (start us, length us, event | category | flops | bytes accessed | tf_op | source)
XLA Modules:
  0.0 130.9 jit_solution(10111388943954427101)
XLA Ops:
  0.6 125.0 %attention_backward.1 = (bf16[1,128,4096]{2,1,0:T(8,128)(2,1)}, bf16[64,512]{1,0:T(8,128)(2,1)}, bf16[64,512]{1,0:T(8,128)(2,1)}, bf16[1,128,512]{2,1,0:T(8,128)(2,1)}, bf16[1,128,512]{2,1,0:T(8,128)(2,1)}) custom-call(bf16[1,128,4096]{2,1,0:T(8,128)(2,1)} %q_hbm.1, bf16[64,512]{1,0:T(8,128)(2,1)} %kp_hbm.1, bf16[64,512]{1,0:T(8,128)(2,1)} %vp_hbm.1, ...), custom_call_target="tpu_custom_call" | custom-call | tf_op jit(solution)/shard_map/attention_backward/pallas_call | solution.py:495
  125.7 0.0 copy-start.3
  125.7 0.0 copy-start.2
  125.7 2.3 %copy.18 = bf16[1,128,4096]{2,1,0:T(8,128)(2,1)} copy(bf16[1,128,4096]{2,1,0:T(8,128)(2,1)} %get-tuple-element.10) | data formatting | bytes 2097152
  128.0 0.0 copy-done.3
  128.0 0.0 copy-start.1
  128.0 0.6 copy.19
  128.6 0.0 copy-done.2
  128.6 0.6 copy.20
  129.3 0.0 copy-done.1
  129.3 0.0 copy-start
  129.3 0.7 copy.21
  129.9 0.3 copy-done
  130.2 0.7 copy.22
Async XLA Ops:
  125.7 2.3 %copy-start.3 = (bf16[64,512]{1,0:T(8,128)(2,1)S(1)}, bf16[64,512]{1,0:T(8,128)(2,1)}, u32[]{:S(2)}) copy-start(bf16[64,512]{1,0:T(8,128)(2,1)} %get-tuple-element.11) | copy-start | bytes 196612
  125.7 3.0 %copy-start.2 = (bf16[64,512]{1,0:T(8,128)(2,1)S(1)}, bf16[64,512]{1,0:T(8,128)(2,1)}, u32[]{:S(2)}) copy-start(bf16[64,512]{1,0:T(8,128)(2,1)} %get-tuple-element.12) | copy-start | bytes 196612
  128.0 1.3 copy-start.1
  129.3 1.0 copy-start

commit v2 on v1

--- a/solution.py
+++ b/solution.py
@@ -14,8 +14,8 @@
 PREFIX = 1024
 WINDOW = 9 * ROWS
 KEYS = PREFIX + WINDOW
-QB = 256
-STEPS = GROUP * ROWS // QB
+QB = 512
+KEPT = PREFIX + 3 * ROWS
 SIDE = 4
 SCALE = DIM ** -0.5
 LOG2E = 1.4426950408889634
@@ -36,59 +36,84 @@
     return op(x.reshape(x.shape[0] // 8, 8, x.shape[1]), axis=0)
 
 
-def attend(h, qb, q_v, do_v, pre, win, bias, live, s_scr, dp_scr, acc, kt, dq_v):
-    col = pl.multiple_of(h * (GROUP * DIM) + qb * QB, QB)
-    qa = q_v[:, pl.ds(col, QB)]
-    da = do_v[:, pl.ds(col, QB)]
-    qs = jnp.concatenate([qa[:, :DIM], qa[:, DIM:]], axis=0)
-    ds_ = jnp.concatenate([da[:, :DIM], da[:, DIM:]], axis=0)
-    chunks = [(256 * i, 256) for i in range(4)] + [(PREFIX + 384 * i, 384) for i in range(3)]
-
-    def rows_of(kv, start, size):
-        if start < PREFIX:
-            return pre[h, kv, pl.ds(start, size), :]
-        return win[h, kv, pl.ds((start - PREFIX) // ROWS, size // ROWS)].reshape(size, DIM)
-
-    top8 = jnp.full((8, QB), MASKED, jnp.float32)
+def head_rows(kv, h, start, size, pre, win):
+    if start < PREFIX:
+        return pre[h, kv, pl.ds(start, size), :]
+    return win[h, kv, pl.ds((start - PREFIX) // ROWS, size // ROWS)].reshape(size, DIM)
+
+
+def stacked(ref, h):
+    parts = [ref[:, pl.ds(pl.multiple_of(h * (GROUP * DIM) + i * DIM, DIM), DIM)] for i in range(GROUP)]
+    return jnp.concatenate(parts, axis=0)
+
+
+def scores(h, half, qt, dot, pre, win, bias, live, s_scr, dp_scr, pb, dsb, slot):
+    cols = pl.ds(half * QB, QB)
+    qs = qt[h, :, cols]
+    gs = dot[h, :, cols]
+    chunks = [(i, ROWS) for i in range(0, KEYS, ROWS)]
+    factor = SCALE * LOG2E
+    stats = []
     for start, size in chunks:
-        s = dot_nt(rows_of(0, start, size), qs)
+        s = dot_nn(head_rows(0, h, start, size, pre, win), qs)
+        dp = dot_nn(head_rows(1, h, start, size, pre, win), gs)
         if start >= PREFIX:
             b = bias[pl.ds(start - PREFIX, size), :]
-            s = s + jnp.concatenate([b, b], axis=1)
-        s_scr[pl.ds(start, size), :] = s
-        top8 = jnp.maximum(top8, fold(s, jnp.max))
-    factor = SCALE * LOG2E
-    shift = jnp.max(top8, axis=0, keepdims=True) * factor
-    sum8 = jnp.zeros((8, QB), jnp.float32)
-    dot8 = jnp.zeros((8, QB), jnp.float32)
-    for start, size in chunks:
-        p = jnp.exp2(s_scr[pl.ds(start, size), :] * factor - shift)
-        dp = dot_nt(rows_of(1, start, size), ds_)
+            s = s + jnp.concatenate([b] * (QB // ROWS), axis=1)
+        top = fold(s, jnp.max) * factor
+        p = jnp.exp2((s * factor).reshape(size // 8, 8, QB) - top[None]).reshape(size, QB)
         s_scr[pl.ds(start, size), :] = p
         dp_scr[pl.ds(start, size), :] = dp
-        sum8 = sum8 + fold(p, jnp.sum)
-        dot8 = dot8 + fold(p * dp, jnp.sum)
-    inverse = 1.0 / jnp.sum(sum8, axis=0, keepdims=True)
-    delta = jnp.sum(dot8, axis=0, keepdims=True) * inverse
+        stats.append((top, fold(p, jnp.sum), fold(p * dp, jnp.sum)))
+    whole = functools.reduce(jnp.maximum, [t for t, _, _ in stats])
+    whole = jnp.max(whole, axis=0, keepdims=True)
+    factors = [jnp.exp2(t - whole) for t, _, _ in stats]
+    total = sum(t[1] * f for t, f in zip(stats, factors))
+    dotted = sum(t[2] * f for t, f in zip(stats, factors))
+    inverse = 1.0 / jnp.sum(total, axis=0, keepdims=True)
+    delta = jnp.sum(dotted, axis=0, keepdims=True) * inverse
     live_row = live[...]
-    inverse = inverse * jnp.concatenate([live_row, live_row], axis=1)
-    dqt = jnp.zeros((DIM, QB), jnp.float32)
-    for start, size in chunks:
-        p = s_scr[pl.ds(start, size), :] * inverse
-        dsc = (p * (dp_scr[pl.ds(start, size), :] - delta)).astype(jnp.bfloat16)
-        pb = p.astype(jnp.bfloat16)
-        acc[h, 1, pl.ds(start, size), :] += dot_nn(pb, ds_)
-        acc[h, 0, pl.ds(start, size), :] += dot_nn(dsc, qs)
-        dqt = dqt + dot_nn(kt[:, pl.ds(start, size)], dsc)
-    dq = (dqt * SCALE).T.astype(jnp.bfloat16)
-    dq_v[:, pl.ds(col, QB)] = jnp.concatenate([dq[:ROWS], dq[ROWS:]], axis=1)
-
-
-def transpose_keys(h, pre, win, kt):
+    inverse = inverse * jnp.concatenate([live_row] * (QB // ROWS), axis=1)
+    for (start, size), f in zip(chunks, factors):
+        rows = pl.ds(start, size)
+        p = (s_scr[rows, :].reshape(size // 8, 8, QB) * (f * inverse)[None]).reshape(size, QB)
+        pb[rows, cols] = p.astype(jnp.bfloat16)
+        dsb[slot, rows, cols] = (p * (dp_scr[rows, :] - delta)).astype(jnp.bfloat16)
+
+
+def prefix_terms(h, q_v, do_v, pb, dsb, acc, slot):
+    rows = pl.ds(0, PREFIX)
+    acc[h, 1, rows, :] = dot_nn(pb[rows, :], stacked(do_v, h))
+    acc[h, 0, rows, :] = dot_nn(dsb[slot, rows, :], stacked(q_v, h))
+
+
+def window_terms(h, q_v, do_v, pb, dsb, acc, rsend, slot):
+    rows = pl.ds(PREFIX, WINDOW)
+    for kv, term in ((1, dot_nn(pb[rows, :], stacked(do_v, h))), (0, dot_nn(dsb[slot, rows, :], stacked(q_v, h)))):
+        for i in range(9):
+            block = term[i * ROWS : (i + 1) * ROWS]
+            rsend[h, i, kv] = block.astype(jnp.bfloat16)
+            if i % 4 == 0:
+                acc[h, kv, pl.ds(PREFIX + (i // 4) * ROWS, ROWS), :] = block
+
+
+def query_terms(h, kt, dsb, dq_v, slot):
+    dq = (dot_nn(kt[slot], dsb[slot]) * SCALE).T.astype(jnp.bfloat16)
+    for i in range(GROUP):
+        dq_v[:, pl.ds(pl.multiple_of(h * (GROUP * DIM) + i * DIM, DIM), DIM)] = dq[i * ROWS : (i + 1) * ROWS]
+
+
+def transpose_keys(h, pre, win, kt, slot):
     for i in range(4):
-        kt[:, pl.ds(256 * i, 256)] = pre[h, 0, pl.ds(256 * i, 256), :].T
+        kt[slot, :, pl.ds(256 * i, 256)] = pre[h, 0, pl.ds(256 * i, 256), :].T
     for i in range(9):
-        kt[:, pl.ds(PREFIX + ROWS * i, ROWS)] = win[h, 0, i].T
+        kt[slot, :, pl.ds(PREFIX + ROWS * i, ROWS)] = win[h, 0, i].T
+
+
+def transpose_queries(ref, out):
+    for h in range(HEADS):
+        for i in range(GROUP):
+            out[h, :, pl.ds(i * DIM, DIM)] = ref[:, pl.ds(h * (GROUP * DIM) + i * DIM, DIM)].T
 
 
 def masks(place, smp, len_ref, asg_ref, bias, live):
@@ -109,9 +134,9 @@
 def kernel(
     q_hbm, kp_hbm, vp_hbm, kr_hbm, vr_hbm, do_hbm, len_ref, asg_ref,
     dq_hbm, dkp_hbm, dvp_hbm, dkr_hbm, dvr_hbm,
-    q_v, do_v, dq_v, pre, win, bias, live, s_scr, dp_scr, acc, kt,
+    q_v, do_v, dq_v, qt, dot, pre, win, bias, live, s_scr, dp_scr, pb, dsb, acc, kt,
     rsend, rrecv, zsend, zrecv,
-    csend, crecv, xsend, xrecv, ysend, yrecv, wsend, wrecv, finall,
+    csend, crecv, xsend, xrecv, ysend, ykept, yrecv, wsend, wrecv, finall,
     okr, okp,
     local, gz_s, gz_r, gy_s, gy_r, pz_s, pz_r, py_s, py_r, px_s, px_r, pc_s, pc_r,
     ry_s, ry_r, rz_s, rz_r, rc_s, rc_r, rx_s, rx_r, rp_s, rp_r, rw_s, rw_r, rf_s, rf_r,
@@ -122,6 +147,8 @@
     x, core = smp // 2, smp % 2
     other = 1 - core
 
+    three = (1, 2, 3)
+
     def at_z(o):
         return {"ctx": ((z + o) % SIDE) * SIDE + y}
 
@@ -138,6 +165,11 @@
             src_ref=src, dst_ref=dst, send_sem=ss, recv_sem=rs, device_id=where, device_id_type=MESH
         )
 
+    barrier = pltpu.get_barrier_semaphore()
+    partners = [at_z(o) for o in (1, 2, 3)] + [at_y(o) for o in (1, 2, 3)]
+    smp_partners = [{"smp": (smp + o) % 8} for o in range(1, 8)]
+    for where in partners + smp_partners:
+        pl.semaphore_signal(barrier, inc=1, device_id=where, device_id_type=MESH)
     loads = []
     for h in range(HEADS):
         cols = pl.ds(h * DIM, DIM)
@@ -169,11 +201,7 @@
     load_q.start()
     load_do.start()
 
-    barrier = pltpu.get_barrier_semaphore()
-    partners = [at_z(o) for o in (1, 2, 3)] + [at_y(o) for o in (1, 2, 3)]
-    smp_partners = [{"smp": (smp + o) % 8} for o in range(1, 8)]
-    for where in partners + smp_partners:
-        pl.semaphore_signal(barrier, inc=1, device_id=where, device_id_type=MESH)
+    masks(ctx, smp, len_ref, asg_ref, bias, live)
     for copy in loads:
         copy.wait()
     for h in range(HEADS):
@@ -181,8 +209,8 @@
     pl.semaphore_wait(barrier, len(partners) + len(smp_partners))
 
     def gather_z(h, step):
-        src, dst = (8, 4) if step == 0 else (4, 0)
-        return send(win.at[h, :, src], win.at[h, :, dst], gz_s.at[h, step], gz_r.at[h, step], at_z(1))
+        dst = 4 - 4 * step
+        return send(win.at[h, :, 8], win.at[h, :, dst], gz_s.at[h, step], gz_r.at[h, step], at_z(1 + step))
 
     def gather_y(h, o, part):
         d = jnp.where(y + o < SIDE, o, o - SIDE)
@@ -194,29 +222,40 @@
 
     def gather_a(h):
         gather_z(h, 0).start()
+        gather_z(h, 1).start()
+
+    def gather_own(h):
+        for o in three:
+            @pl.when(y + o < SIDE)
+            def _():
+                gather_y(h, o, 1).start()
 
     def gather_b(h):
         gather_z(h, 0).wait_recv()
-        gather_z(h, 1).start()
-        for o in (1, 2, 3):
+        for o in three:
             gather_y(h, o, 0).start()
-
-    def gather_c(h):
         gather_z(h, 1).wait_recv()
-        for o in (1, 2, 3):
-            gather_y(h, o, 1).start()
+        for o in three:
+            @pl.when(y + o >= SIDE)
+            def _():
+                gather_y(h, o, 1).start()
 
     def gather_d(h):
         for o in (1, 2, 3):
             gather_y(h, o, 0).wait_recv()
             gather_y(h, o, 1).wait_recv()
 
-    def prefix_z(o):
-        return send(pre.at[:, core, mine, :], pre.at[:, core, mine, :], pz_s.at[o - 1], pz_r.at[o - 1], at_z(o))
-
-    def prefix_y(o):
+    def some(h):
+        return pl.ds(0, 1) if h == 0 else pl.ds(1, HEADS - 1)
+
+    def prefix_z(h, o):
+        part = pre.at[some(h), core, mine, :]
+        return send(part, part, pz_s.at[h, o - 1], pz_r.at[h, o - 1], at_z(o))
+
+    def prefix_y(h, o):
         rows = pl.ds(pl.multiple_of(x * 256 + y * 64, 64), 64)
-        return send(pre.at[:, core, rows, :], pre.at[:, core, rows, :], py_s.at[o - 1], py_r.at[o - 1], at_y(o))
+        part = pre.at[some(h), core, rows, :]
+        return send(part, part, py_s.at[h, o - 1], py_r.at[h, o - 1], at_y(o))
 
     def prefix_x(h, o):
         rows = pl.ds(pl.multiple_of(x * 256, 256), 256)
@@ -240,15 +279,12 @@
         )
 
     def reduce_z(h, step):
-        return send(zsend.at[h, step], zrecv.at[h, step], rz_s.at[h, step], rz_r.at[h, step], at_z(3))
+        return send(zsend.at[h, step], zrecv.at[h, step], rz_s.at[h, step], rz_r.at[h, step], at_z(3 - step))
 
     def slot_rows(i):
-        return pl.ds(PREFIX + i * ROWS, ROWS)
+        return pl.ds(PREFIX + (i // 4) * ROWS, ROWS)
 
     def reduce_a(h):
-        for i in range(9):
-            for kv in range(2):
-                rsend[h, i, kv] = acc[h, kv, slot_rows(i), :].astype(jnp.bfloat16)
         for o in (1, 2, 3):
             for part in (1, 0):
                 reduce_y(h, o, part).start()
@@ -267,22 +303,19 @@
                 lower = jnp.where(y >= o, 1.0, 0.0).astype(jnp.float32)
                 far = far + term * lower
                 near = near + term * (1.0 - lower)
-            zsend[h, 0, kv] = far.astype(jnp.bfloat16)
-            acc[h, kv, slot_rows(4), :] = mid
+            zsend[h, 0, kv] = mid.astype(jnp.bfloat16)
+            zsend[h, 1, kv] = far.astype(jnp.bfloat16)
             acc[h, kv, slot_rows(8), :] = near
+        reduce_z(h, 1).start()
         reduce_z(h, 0).start()
 
     def reduce_c(h):
         reduce_z(h, 0).wait_recv()
-        for kv in range(2):
-            mid = acc[h, kv, slot_rows(4), :] + zrecv[h, 0, kv].astype(jnp.float32)
-            zsend[h, 1, kv] = mid.astype(jnp.bfloat16)
-        reduce_z(h, 1).start()
-
-    def reduce_d(h):
         reduce_z(h, 1).wait_recv()
         for kv in range(2):
-            near = acc[h, kv, slot_rows(8), :] + zrecv[h, 1, kv].astype(jnp.float32)
+            near = acc[h, kv, slot_rows(8), :]
+            for step in range(2):
+                near = near + zrecv[h, step, kv].astype(jnp.float32)
             if kv == 0:
                 near = near * SCALE
             okr[kv, h] = near.astype(jnp.bfloat16)
@@ -325,16 +358,17 @@
         whole = acc[h, core, pl.ds(pl.multiple_of(x * 256, 256), 256), :]
         for o in (1, 2, 3):
             whole = whole + xrecv[h, o - 1].astype(jnp.float32)
-        ysend[h] = whole.reshape(SIDE, 64, DIM)
+        ysend[h] = whole.astype(jnp.bfloat16).reshape(SIDE, 64, DIM)
+        ykept[h] = whole.reshape(SIDE, 64, DIM)
         for o in (1, 2, 3):
             total_y(h, o).start()
 
     def total_e(h):
         for o in (1, 2, 3):
             total_y(h, o).wait_recv()
-        whole = ysend[h, y]
-        for o in (1, 2, 3):
-            whole = whole + yrecv[h, o - 1]
+        whole = ykept[h, y]
+        for o in (1, 2, 3):
+            whole = whole + yrecv[h, o - 1].astype(jnp.float32)
         wsend[h] = whole.reshape(SIDE, 16, DIM)
         for o in (1, 2, 3):
             total_z(h, o).start()
@@ -351,95 +385,113 @@
     def total_g(o):
         return send(finall.at[smp], finall.at[smp], rf_s.at[o - 1], rf_r.at[o - 1], smp_partners[o - 1])
 
-    for o in (1, 2, 3):
-        prefix_z(o).start()
+    for part in range(2):
+        for o in three:
+            prefix_z(part, o).start()
     gather_a(0)
-    masks(ctx, smp, len_ref, asg_ref, bias, live)
-    for o in (1, 2, 3):
-        prefix_z(o).wait_recv()
-    for o in (1, 2, 3):
-        prefix_y(o).start()
-    gather_b(0)
-    gather_a(1)
-    acc[...] = jnp.zeros_like(acc)
-    for o in (1, 2, 3):
-        prefix_y(o).wait_recv()
-    for h in range(HEADS):
-        for o in (1, 2, 3):
-            prefix_x(h, o).start()
+    gather_own(0)
     load_q.wait()
     load_do.wait()
-    gather_c(0)
+    transpose_queries(q_v, qt)
+    for part in range(2):
+        for o in three:
+            prefix_z(part, o).wait_recv()
+        for o in three:
+            prefix_y(part, o).start()
+    gather_own(1)
+    gather_a(1)
+    transpose_queries(do_v, dot)
+    for o in three:
+        prefix_y(0, o).wait_recv()
+    for o in three:
+        prefix_x(0, o).start()
+    gather_b(0)
+    for o in three:
+        prefix_y(1, o).wait_recv()
+    for o in three:
+        prefix_x(1, o).start()
+    gather_own(2)
+    gather_own(3)
+    gather_a(2)
     prefix_last(0)
     gather_b(1)
-    gather_a(2)
+    for h in range(2, HEADS):
+        for o in three:
+            prefix_x(h, o).start()
     gather_d(0)
     prefix_c(0).wait_recv()
 
-    @pl.loop(0, HEADS * STEPS)
-    def _(it):
-        h, qb = it // STEPS, it % STEPS
-
-        @pl.when((qb == 0) & (h > 0))
+    @pl.loop(0, HEADS)
+    def _(h):
+        @pl.when(h > 0)
         def _():
             gather_d(h)
             prefix_c(h).wait_recv()
 
-        @pl.when(qb == 0)
-        def _():
-            transpose_keys(h, pre, win, kt)
-
-        attend(h, qb, q_v, do_v, pre, win, bias, live, s_scr, dp_scr, acc, kt, dq_v)
-
-        @pl.when((qb == 0) & (h > 0))
+        @pl.when(h == 0)
+        def _():
+            gather_a(3)
+
+        transpose_keys(h, pre, win, kt, h)
+        scores(h, 0, qt, dot, pre, win, bias, live, s_scr, dp_scr, pb, dsb, h)
+
+        @pl.when(h > 0)
         def _():
             total_b(h - 1)
-            reduce_b(h - 1)
-
-        @pl.when((qb == 0) & (h + 1 < HEADS))
-        def _():
-            gather_c(h + 1)
+
+        @pl.when(h + 1 < HEADS)
+        def _():
             prefix_last(h + 1)
 
-        @pl.when((qb == 1) & (h + 2 < HEADS))
+        @pl.when(h + 2 < HEADS)
         def _():
             gather_b(h + 2)
 
-        @pl.when((qb == 1) & (h + 3 < HEADS))
-        def _():
-            gather_a(h + 3)
-
-        @pl.when((qb == 1) & (h > 0))
-        def _():
-            total_d(h - 1)
-            reduce_c(h - 1)
-
-        @pl.when((qb == 2) & (h > 0))
-        def _():
-            total_e(h - 1)
-            reduce_d(h - 1)
-
-        @pl.when((qb == 3) & (h > 0))
-        def _():
-            total_f(h - 1)
-
-        @pl.when(qb == STEPS - 1)
-        def _():
-            total_a(h)
-            reduce_a(h)
-
+        @pl.when(h > 1)
+        def _():
+            total_d(h - 2)
+            reduce_b(h - 2)
+
+        scores(h, 1, qt, dot, pre, win, bias, live, s_scr, dp_scr, pb, dsb, h)
+
+        @pl.when(h > 2)
+        def _():
+            total_f(h - 3)
+
+        prefix_terms(h, q_v, do_v, pb, dsb, acc, h)
+        total_a(h)
+        window_terms(h, q_v, do_v, pb, dsb, acc, rsend, h)
+        reduce_a(h)
+
+        @pl.when(h > 1)
+        def _():
+            total_e(h - 2)
+
+        @pl.when(h > 2)
+        def _():
+            reduce_c(h - 3)
+
+    query_terms(0, kt, dsb, dq_v, 0)
+    total_d(2)
+    total_b(3)
+    reduce_b(2)
+    query_terms(1, kt, dsb, dq_v, 1)
+    query_terms(2, kt, dsb, dq_v, 2)
+    total_f(1)
+    total_e(2)
+    query_terms(3, kt, dsb, dq_v, 3)
     store_q = pltpu.make_async_copy(dq_v, dq_hbm.at[0], local.at[12])
     store_q.start()
-    last = HEADS - 1
-    total_b(last)
-    reduce_b(last)
-    total_d(last)
-    reduce_c(last)
-    total_e(last)
-    total_f(last)
+    total_d(3)
+    reduce_b(3)
+    reduce_c(1)
+    total_e(3)
+    total_f(2)
+    reduce_c(2)
+    total_f(3)
     for o in range(1, 8):
         total_g(o).start()
-    reduce_d(last)
+    reduce_c(3)
     stores = []
     for h in range(HEADS):
         cols = pl.ds(h * DIM, DIM)
@@ -460,9 +512,10 @@
     for copy in tail:
         copy.start()
 
-    for o in (1, 2, 3):
-        prefix_z(o).wait_send()
-        prefix_y(o).wait_send()
+    for o in three:
+        for h in range(2):
+            prefix_z(h, o).wait_send()
+            prefix_y(h, o).wait_send()
     for o in range(1, 8):
         total_g(o).wait_send()
 
@@ -486,13 +539,26 @@
         copy.wait()
 
 
+def hand_over(*refs):
+    ins, outs, held, sems = refs[:5], refs[5:10], refs[10:15], refs[15]
+    first = [pltpu.make_async_copy(ins[i], held[i], sems.at[i]) for i in range(5)]
+    second = [pltpu.make_async_copy(held[i], outs[i], sems.at[i]) for i in range(5)]
+    for copy in first:
+        copy.start()
+    for a, b in zip(first, second):
+        a.wait()
+        b.start()
+    for copy in second:
+        copy.wait()
+
+
 def shards(q, kp, vp, kr, vr, do, lengths, assign):
     bf, f32 = jnp.bfloat16, jnp.float32
     dma = pltpu.SemaphoreType.DMA
     hbm = pl.BlockSpec(memory_space=pl.ANY)
     smem = pl.BlockSpec(memory_space=pltpu.SMEM)
     H = HEADS
-    return pl.pallas_call(
+    outs = pl.pallas_call(
         kernel,
         out_shape=(
             jax.ShapeDtypeStruct(q.shape, bf),
@@ -507,14 +573,18 @@
             pltpu.VMEM((ROWS, H * GROUP * DIM), bf),
             pltpu.VMEM((ROWS, H * GROUP * DIM), bf),
             pltpu.VMEM((ROWS, H * GROUP * DIM), bf),
+            pltpu.VMEM((H, DIM, GROUP * ROWS), bf),
+            pltpu.VMEM((H, DIM, GROUP * ROWS), bf),
             pltpu.VMEM((H, 2, PREFIX, DIM), bf),
             pltpu.VMEM((H, 2, 9, ROWS, DIM), bf),
             pltpu.VMEM((WINDOW, ROWS), f32),
             pltpu.VMEM((1, ROWS), f32),
             pltpu.VMEM((KEYS, QB), f32),
             pltpu.VMEM((KEYS, QB), f32),
-            pltpu.VMEM((H, 2, KEYS, DIM), f32),
-            pltpu.VMEM((DIM, KEYS), bf),
+            pltpu.VMEM((KEYS, GROUP * ROWS), bf),
+            pltpu.VMEM((H, KEYS, GROUP * ROWS), bf),
+            pltpu.VMEM((H, 2, KEPT, DIM), f32),
+            pltpu.VMEM((H, DIM, KEYS), bf),
             pltpu.VMEM((H, 9, 2, ROWS, DIM), bf),
             pltpu.VMEM((H, 3, 2, 2, ROWS, DIM), bf),
             pltpu.VMEM((H, 2, 2, ROWS, DIM), bf),
@@ -523,8 +593,9 @@
             pltpu.VMEM((H, PREFIX, DIM), bf),
             pltpu.VMEM((H, SIDE, 256, DIM), bf),
             pltpu.VMEM((H, 3, 256, DIM), bf),
+            pltpu.VMEM((H, SIDE, 64, DIM), bf),
             pltpu.VMEM((H, SIDE, 64, DIM), f32),
-            pltpu.VMEM((H, 3, 64, DIM), f32),
+            pltpu.VMEM((H, 3, 64, DIM), bf),
             pltpu.VMEM((H, SIDE, 16, DIM), f32),
             pltpu.VMEM((H, 3, 16, DIM), f32),
             pltpu.VMEM((8, H, 16, DIM), bf),
@@ -532,7 +603,7 @@
             pltpu.VMEM((2, 64, H * DIM), bf),
             dma((14,)),
             dma((H, 2)), dma((H, 2)), dma((H, 3, 2)), dma((H, 3, 2)),
-            dma((3,)), dma((3,)), dma((3,)), dma((3,)),
+            dma((2, 3)), dma((2, 3)), dma((2, 3)), dma((2, 3)),
             dma((H, 3)), dma((H, 3)), dma((H,)), dma((H,)),
             dma((H, 3, 2)), dma((H, 3, 2)), dma((H, 2)), dma((H, 2)),
             dma((H,)), dma((H,)), dma((H, 3)), dma((H, 3)),
@@ -540,10 +611,19 @@
             dma((7,)), dma((7,)),
         ],
         compiler_params=pltpu.CompilerParams(
-            collective_id=0, has_side_effects=True, vmem_limit_bytes=56 * 1024 * 1024
+            collective_id=0, has_side_effects=True, vmem_limit_bytes=63 * 1024 * 1024
         ),
         name="attention_backward",
     )(q, kp, vp, kr, vr, do, lengths, assign)
+    return pl.pallas_call(
+        hand_over,
+        out_shape=tuple(jax.ShapeDtypeStruct(o.shape, o.dtype) for o in outs),
+        in_specs=[hbm] * 5,
+        out_specs=(hbm,) * 5,
+        scratch_shapes=[pltpu.VMEM(o.shape, o.dtype) for o in outs] + [dma((5,))],
+        compiler_params=pltpu.CompilerParams(vmem_limit_bytes=63 * 1024 * 1024),
+        name="hand_over",
+    )(*outs)
 
 
 def solution(mesh):

time: 131 us -> 95.3 us (0.73)
  Pallas kernels: 125 us -> 94.6 us
  local copies, waits for them, and re-layouts: 5.2 us -> 0 us
    pallas_call x1, Pallas kernels: 125 us -> 92.2 us  [shards(): pl.pallas_call(kernel, out_shape=(jax.ShapeDtypeStruct(q.shape, bf), jax....]
    unnamed x13 -> x0, local copies, waits for them, and re-layouts: 5.2 us -> none
    pallas_call x0 -> x1, Pallas kernels: none -> 2.35 us  [shards(): pl.pallas_call(hand_over, out_shape=tuple((jax.ShapeDtypeStruct(o.shape,...]
where the time goes in v2:
time: 95.3 us; the launch traced here: 95.2 us
  Pallas kernels  94.6 us (99%)
    pallas_call x1, Pallas kernels, shards(): pl.pallas_call(kernel, out_shape=(jax.ShapeDtypeStruct(q.shape, bf), jax....  92.2 us
    pallas_call x1, Pallas kernels, shards(): pl.pallas_call(hand_over, out_shape=tuple((jax.ShapeDtypeStruct(o.shape,...  2.35 us

profile of v2, /device:TPU:1, one launch (start us, length us, event | category | flops | bytes accessed | tf_op | source)
XLA Modules:
  0.0 95.2 jit_solution(14964764426949280777)
XLA Ops:
  0.6 92.2 %attention_backward.1 = (bf16[1,128,4096]{2,1,0:T(8,128)(2,1)}, bf16[64,512]{1,0:T(8,128)(2,1)}, bf16[64,512]{1,0:T(8,128)(2,1)}, bf16[1,128,512]{2,1,0:T(8,128)(2,1)}, bf16[1,128,512]{2,1,0:T(8,128)(2,1)}) custom-call(bf16[1,128,4096]{2,1,0:T(8,128)(2,1)} %q_hbm.1, bf16[64,512]{1,0:T(8,128)(2,1)} %kp_hbm.1, bf16[64,512]{1,0:T(8,128)(2,1)} %vp_hbm.1, ...), custom_call_target="tpu_custom_call" | custom-call | tf_op jit(solution)/shard_map/attention_backward/pallas_call | solution.py:561
  92.8 2.4 %hand_over.1 = (bf16[1,128,4096]{2,1,0:T(8,128)(2,1)}, bf16[64,512]{1,0:T(8,128)(2,1)}, bf16[64,512]{1,0:T(8,128)(2,1)}, bf16[1,128,512]{2,1,0:T(8,128)(2,1)}, bf16[1,128,512]{2,1,0:T(8,128)(2,1)}) custom-call(bf16[1,128,4096]{2,1,0:T(8,128)(2,1)} %get-tuple-element.10.refs_0_, bf16[64,512]{1,0:T(8,128)(2,1)} %get-tuple-element.11.refs_1_, ...), custom_call_target="tpu_custom_call" | custom-call | tf_op jit(solution)/shard_map/hand_over/pallas_call | solution.py:618

commit v3 on v2

--- a/solution.py
+++ b/solution.py
@@ -39,7 +39,8 @@
 def head_rows(kv, h, start, size, pre, win):
     if start < PREFIX:
         return pre[h, kv, pl.ds(start, size), :]
-    return win[h, kv, pl.ds((start - PREFIX) // ROWS, size // ROWS)].reshape(size, DIM)
+    i = (start - PREFIX) // ROWS
+    return win[h, kv, i // 4, i % 4]
 
 
 def stacked(ref, h):
@@ -48,7 +49,7 @@
 
 
 def scores(h, half, qt, dot, pre, win, bias, live, s_scr, dp_scr, pb, dsb, slot):
-    cols = pl.ds(half * QB, QB)
+    cols = pl.ds(pl.multiple_of(half * QB, QB), QB)
     qs = qt[h, :, cols]
     gs = dot[h, :, cols]
     chunks = [(i, ROWS) for i in range(0, KEYS, ROWS)]
@@ -92,7 +93,7 @@
     for kv, term in ((1, dot_nn(pb[rows, :], stacked(do_v, h))), (0, dot_nn(dsb[slot, rows, :], stacked(q_v, h)))):
         for i in range(9):
             block = term[i * ROWS : (i + 1) * ROWS]
-            rsend[h, i, kv] = block.astype(jnp.bfloat16)
+            rsend[h, i // 4, i % 4, kv] = block.astype(jnp.bfloat16)
             if i % 4 == 0:
                 acc[h, kv, pl.ds(PREFIX + (i // 4) * ROWS, ROWS), :] = block
 
@@ -107,7 +108,7 @@
     for i in range(4):
         kt[slot, :, pl.ds(256 * i, 256)] = pre[h, 0, pl.ds(256 * i, 256), :].T
     for i in range(9):
-        kt[slot, :, pl.ds(PREFIX + ROWS * i, ROWS)] = win[h, 0, i].T
+        kt[slot, :, pl.ds(PREFIX + ROWS * i, ROWS)] = win[h, 0, i // 4, i % 4].T
 
 
 def transpose_queries(ref, out):
@@ -134,7 +135,7 @@
 def kernel(
     q_hbm, kp_hbm, vp_hbm, kr_hbm, vr_hbm, do_hbm, len_ref, asg_ref,
     dq_hbm, dkp_hbm, dvp_hbm, dkr_hbm, dvr_hbm,
-    q_v, do_v, dq_v, qt, dot, pre, win, bias, live, s_scr, dp_scr, pb, dsb, acc, kt,
+    q_v, do_v, qt, dot, pre, win, bias, live, s_scr, dp_scr, pb, dsb, acc, kt,
     rsend, rrecv, zsend, zrecv,
     csend, crecv, xsend, xrecv, ysend, ykept, yrecv, wsend, wrecv, finall,
     okr, okp,
@@ -173,8 +174,8 @@
     loads = []
     for h in range(HEADS):
         cols = pl.ds(h * DIM, DIM)
-        loads.append(pltpu.make_async_copy(kr_hbm.at[0, :, cols], win.at[h, 0, 8], local.at[2 * h]))
-        loads.append(pltpu.make_async_copy(vr_hbm.at[0, :, cols], win.at[h, 1, 8], local.at[2 * h + 1]))
+        loads.append(pltpu.make_async_copy(kr_hbm.at[0, :, cols], win.at[h, 0, 2, 0], local.at[2 * h]))
+        loads.append(pltpu.make_async_copy(vr_hbm.at[0, :, cols], win.at[h, 1, 2, 0], local.at[2 * h + 1]))
     mine = pl.ds(pl.multiple_of(x * 256 + y * 64 + z * 16, 16), 16)
     from_rows = pl.ds(pl.multiple_of(x * 16, 16), 16)
 
@@ -209,41 +210,28 @@
     pl.semaphore_wait(barrier, len(partners) + len(smp_partners))
 
     def gather_z(h, step):
-        dst = 4 - 4 * step
-        return send(win.at[h, :, 8], win.at[h, :, dst], gz_s.at[h, step], gz_r.at[h, step], at_z(1 + step))
-
-    def gather_y(h, o, part):
-        d = jnp.where(y + o < SIDE, o, o - SIDE)
-        if part == 0:
-            src, dst = 4, 4 - d
-        else:
-            src, dst = jnp.where(d > 0, 8, 0), jnp.where(d > 0, 8 - d, -d)
-        return send(win.at[h, :, src], win.at[h, :, dst], gy_s.at[h, o - 1, part], gy_r.at[h, o - 1, part], at_y(o))
+        return send(win.at[h, :, 2, 0], win.at[h, :, 1 - step, 0], gz_s.at[h, step], gz_r.at[h, step], at_z(1 + step))
+
+    def gather_y(h, o):
+        later = jnp.where(y + o < SIDE, 1, 0)
+        return send(
+            win.at[h, :, pl.ds(later, 2), 0], win.at[h, :, pl.ds(0, 2), SIDE - o],
+            gy_s.at[h, o - 1], gy_r.at[h, o - 1], at_y(o),
+        )
 
     def gather_a(h):
         gather_z(h, 0).start()
         gather_z(h, 1).start()
 
-    def gather_own(h):
-        for o in three:
-            @pl.when(y + o < SIDE)
-            def _():
-                gather_y(h, o, 1).start()
-
     def gather_b(h):
         gather_z(h, 0).wait_recv()
-        for o in three:
-            gather_y(h, o, 0).start()
         gather_z(h, 1).wait_recv()
         for o in three:
-            @pl.when(y + o >= SIDE)
-            def _():
-                gather_y(h, o, 1).start()
+            gather_y(h, o).start()
 
     def gather_d(h):
         for o in (1, 2, 3):
-            gather_y(h, o, 0).wait_recv()
-            gather_y(h, o, 1).wait_recv()
+            gather_y(h, o).wait_recv()
 
     def some(h):
         return pl.ds(0, 1) if h == 0 else pl.ds(1, HEADS - 1)
@@ -271,11 +259,9 @@
             prefix_x(h, o).wait_recv()
         prefix_c(h).start()
 
-    def reduce_y(h, o, part):
-        d = jnp.where(y + o < SIDE, o, o - SIDE)
-        src = 4 + d if part == 0 else jnp.where(d > 0, d, 8 + d)
+    def reduce_y(h, o):
         return send(
-            rsend.at[h, src], rrecv.at[h, o - 1, part], ry_s.at[h, o - 1, part], ry_r.at[h, o - 1, part], at_y(o)
+            rsend.at[h, pl.ds(0, 2), o], rrecv.at[h, o - 1], ry_s.at[h, o - 1], ry_r.at[h, o - 1], at_y(o)
         )
 
     def reduce_z(h, step):
@@ -286,23 +272,22 @@
 
     def reduce_a(h):
         for o in (1, 2, 3):
-            for part in (1, 0):
-                reduce_y(h, o, part).start()
+            reduce_y(h, o).start()
 
     def reduce_b(h):
         for o in (1, 2, 3):
-            reduce_y(h, o, 0).wait_recv()
-            reduce_y(h, o, 1).wait_recv()
+            reduce_y(h, o).wait_recv()
         for kv in range(2):
             far = acc[h, kv, slot_rows(0), :]
             mid = acc[h, kv, slot_rows(4), :]
             near = acc[h, kv, slot_rows(8), :]
             for o in (1, 2, 3):
-                mid = mid + rrecv[h, o - 1, 0, kv].astype(jnp.float32)
-                term = rrecv[h, o - 1, 1, kv].astype(jnp.float32)
+                one = rrecv[h, o - 1, 0, kv].astype(jnp.float32)
+                two = rrecv[h, o - 1, 1, kv].astype(jnp.float32)
                 lower = jnp.where(y >= o, 1.0, 0.0).astype(jnp.float32)
-                far = far + term * lower
-                near = near + term * (1.0 - lower)
+                far = far + one * lower
+                near = near + two * (1.0 - lower)
+                mid = mid + two * lower + one * (1.0 - lower)
             zsend[h, 0, kv] = mid.astype(jnp.bfloat16)
             zsend[h, 1, kv] = far.astype(jnp.bfloat16)
             acc[h, kv, slot_rows(8), :] = near
@@ -389,7 +374,6 @@
         for o in three:
             prefix_z(part, o).start()
     gather_a(0)
-    gather_own(0)
     load_q.wait()
     load_do.wait()
     transpose_queries(q_v, qt)
@@ -398,7 +382,6 @@
             prefix_z(part, o).wait_recv()
         for o in three:
             prefix_y(part, o).start()
-    gather_own(1)
     gather_a(1)
     transpose_queries(do_v, dot)
     for o in three:
@@ -410,8 +393,6 @@
         prefix_y(1, o).wait_recv()
     for o in three:
         prefix_x(1, o).start()
-    gather_own(2)
-    gather_own(3)
     gather_a(2)
     prefix_last(0)
     gather_b(1)
@@ -421,73 +402,108 @@
     gather_d(0)
     prefix_c(0).wait_recv()
 
+    @pl.loop(0, 2 * HEADS)
+    def _(it):
+        h, half = it // 2, it % 2
+
+        @pl.when(half == 0)
+        def _():
+            @pl.when(h > 0)
+            def _():
+                gather_d(h)
+                prefix_c(h).wait_recv()
+
+            @pl.when(h == 0)
+            def _():
+                gather_a(3)
+
+            transpose_keys(h, pre, win, kt, h)
+
+        scores(h, half, qt, dot, pre, win, bias, live, s_scr, dp_scr, pb, dsb, h)
+
+        @pl.when(half == 0)
+        def _():
+            @pl.when(h > 0)
+            def _():
+                total_b(h - 1)
+
+            @pl.when(h + 1 < HEADS)
+            def _():
+                prefix_last(h + 1)
+
+            @pl.when(h + 2 < HEADS)
+            def _():
+                gather_b(h + 2)
+
+            @pl.when(h > 1)
+            def _():
+                total_d(h - 2)
+                reduce_b(h - 2)
+
+        @pl.when(half == 1)
+        def _():
+            prefix_terms(h, q_v, do_v, pb, dsb, acc, h)
+            total_a(h)
+            window_terms(h, q_v, do_v, pb, dsb, acc, rsend, h)
+            reduce_a(h)
+
+            @pl.when(h == HEADS - 1)
+            def _():
+                total_b(h)
+
+            @pl.when(h > 2)
+            def _():
+                total_f(h - 3)
+
+            @pl.when(h > 1)
+            def _():
+                total_e(h - 2)
+
+            @pl.when(h > 2)
+            def _():
+                reduce_c(h - 3)
+
+    total_d(2)
+    query_terms(0, kt, dsb, q_v, 0)
+    reduce_b(2)
+    query_terms(1, kt, dsb, q_v, 1)
+    query_terms(2, kt, dsb, q_v, 2)
+    total_e(2)
+    query_terms(3, kt, dsb, q_v, 3)
+    store_q = pltpu.make_async_copy(q_v, dq_hbm.at[0], local.at[12])
+    store_q.start()
+    total_d(3)
+    total_f(1)
+    for o in three:
+        for h in range(2):
+            prefix_z(h, o).wait_send()
+            prefix_y(h, o).wait_send()
+    reduce_b(3)
+    reduce_c(1)
+
     @pl.loop(0, HEADS)
     def _(h):
-        @pl.when(h > 0)
-        def _():
-            gather_d(h)
-            prefix_c(h).wait_recv()
-
-        @pl.when(h == 0)
-        def _():
-            gather_a(3)
-
-        transpose_keys(h, pre, win, kt, h)
-        scores(h, 0, qt, dot, pre, win, bias, live, s_scr, dp_scr, pb, dsb, h)
-
-        @pl.when(h > 0)
-        def _():
-            total_b(h - 1)
-
-        @pl.when(h + 1 < HEADS)
-        def _():
-            prefix_last(h + 1)
-
-        @pl.when(h + 2 < HEADS)
-        def _():
-            gather_b(h + 2)
-
-        @pl.when(h > 1)
-        def _():
-            total_d(h - 2)
-            reduce_b(h - 2)
-
-        scores(h, 1, qt, dot, pre, win, bias, live, s_scr, dp_scr, pb, dsb, h)
-
-        @pl.when(h > 2)
-        def _():
-            total_f(h - 3)
-
-        prefix_terms(h, q_v, do_v, pb, dsb, acc, h)
-        total_a(h)
-        window_terms(h, q_v, do_v, pb, dsb, acc, rsend, h)
-        reduce_a(h)
-
-        @pl.when(h > 1)
-        def _():
-            total_e(h - 2)
-
-        @pl.when(h > 2)
-        def _():
-            reduce_c(h - 3)
-
-    query_terms(0, kt, dsb, dq_v, 0)
-    total_d(2)
-    total_b(3)
-    reduce_b(2)
-    query_terms(1, kt, dsb, dq_v, 1)
-    query_terms(2, kt, dsb, dq_v, 2)
-    total_f(1)
-    total_e(2)
-    query_terms(3, kt, dsb, dq_v, 3)
-    store_q = pltpu.make_async_copy(dq_v, dq_hbm.at[0], local.at[12])
-    store_q.start()
-    total_d(3)
-    reduce_b(3)
-    reduce_c(1)
+        prefix_c(h).wait_send()
+        for step in range(2):
+            gather_z(h, step).wait_send()
+        for o in three:
+            prefix_x(h, o).wait_send()
+            gather_y(h, o).wait_send()
+
     total_e(3)
     total_f(2)
     reduce_c(2)
+
+    @pl.loop(0, HEADS)
+    def _(h):
+        total_c(h).wait_send()
+        for step in range(2):
+            reduce_z(h, step).wait_send()
+        for o in three:
+            total_x(h, o).wait_send()
+            total_y(h, o).wait_send()
+            reduce_y(h, o).wait_send()
+
     total_f(3)
     for o in range(1, 8):
         total_g(o).start()
@@ -512,28 +528,13 @@
     for copy in tail:
         copy.start()
 
-    for o in three:
-        for h in range(2):
-            prefix_z(h, o).wait_send()
-            prefix_y(h, o).wait_send()
     for o in range(1, 8):
         total_g(o).wait_send()
 
     @pl.loop(0, HEADS)
     def _(h):
-        prefix_c(h).wait_send()
-        total_c(h).wait_send()
-        for step in range(2):
-            gather_z(h, step).wait_send()
-            reduce_z(h, step).wait_send()
-        for o in (1, 2, 3):
-            prefix_x(h, o).wait_send()
-            total_x(h, o).wait_send()
-            total_y(h, o).wait_send()
+        for o in three:
             total_z(h, o).wait_send()
-            for part in range(2):
-                gather_y(h, o, part).wait_send()
-                reduce_y(h, o, part).wait_send()
 
     for copy in stores + tail + [store_q]:
         copy.wait()
@@ -572,11 +573,10 @@
         scratch_shapes=[
             pltpu.VMEM((ROWS, H * GROUP * DIM), bf),
             pltpu.VMEM((ROWS, H * GROUP * DIM), bf),
-            pltpu.VMEM((ROWS, H * GROUP * DIM), bf),
             pltpu.VMEM((H, DIM, GROUP * ROWS), bf),
             pltpu.VMEM((H, DIM, GROUP * ROWS), bf),
             pltpu.VMEM((H, 2, PREFIX, DIM), bf),
-            pltpu.VMEM((H, 2, 9, ROWS, DIM), bf),
+            pltpu.VMEM((H, 2, 3, 4, ROWS, DIM), bf),
             pltpu.VMEM((WINDOW, ROWS), f32),
             pltpu.VMEM((1, ROWS), f32),
             pltpu.VMEM((KEYS, QB), f32),
@@ -585,7 +585,7 @@
             pltpu.VMEM((H, KEYS, GROUP * ROWS), bf),
             pltpu.VMEM((H, 2, KEPT, DIM), f32),
             pltpu.VMEM((H, DIM, KEYS), bf),
-            pltpu.VMEM((H, 9, 2, ROWS, DIM), bf),
+            pltpu.VMEM((H, 3, 4, 2, ROWS, DIM), bf),
             pltpu.VMEM((H, 3, 2, 2, ROWS, DIM), bf),
             pltpu.VMEM((H, 2, 2, ROWS, DIM), bf),
             pltpu.VMEM((H, 2, 2, ROWS, DIM), bf),
@@ -602,10 +602,10 @@
             pltpu.VMEM((2, H, ROWS, DIM), bf),
             pltpu.VMEM((2, 64, H * DIM), bf),
             dma((14,)),
-            dma((H, 2)), dma((H, 2)), dma((H, 3, 2)), dma((H, 3, 2)),
+            dma((H, 2)), dma((H, 2)), dma((H, 3)), dma((H, 3)),
             dma((2, 3)), dma((2, 3)), dma((2, 3)), dma((2, 3)),
             dma((H, 3)), dma((H, 3)), dma((H,)), dma((H,)),
-            dma((H, 3, 2)), dma((H, 3, 2)), dma((H, 2)), dma((H, 2)),
+            dma((H, 3)), dma((H, 3)), dma((H, 2)), dma((H, 2)),
             dma((H,)), dma((H,)), dma((H, 3)), dma((H, 3)),
             dma((H, 3)), dma((H, 3)), dma((H, 3)), dma((H, 3)),
             dma((7,)), dma((7,)),

time: 95.3 us -> 94.7 us (level)
  no operation moved by 1% of the time
where the time goes in v3:
time: 94.7 us; the launch traced here: 94.5 us
  Pallas kernels  93.9 us (99%)
    pallas_call x1, Pallas kernels, shards(): pl.pallas_call(kernel, out_shape=(jax.ShapeDtypeStruct(q.shape, bf), jax....  91.5 us
    pallas_call x1, Pallas kernels, shards(): pl.pallas_call(hand_over, out_shape=tuple((jax.ShapeDtypeStruct(o.shape,...  2.35 us

profile of v3, /device:TPU:1, one launch (start us, length us, event | category | flops | bytes accessed | tf_op | source)
XLA Modules:
  0.0 94.5 jit_solution(12249010865629478684)
XLA Ops:
  0.6 91.5 %attention_backward.1 = (bf16[1,128,4096]{2,1,0:T(8,128)(2,1)}, bf16[64,512]{1,0:T(8,128)(2,1)}, bf16[64,512]{1,0:T(8,128)(2,1)}, bf16[1,128,512]{2,1,0:T(8,128)(2,1)}, bf16[1,128,512]{2,1,0:T(8,128)(2,1)}) custom-call(bf16[1,128,4096]{2,1,0:T(8,128)(2,1)} %q_hbm.1, bf16[64,512]{1,0:T(8,128)(2,1)} %kp_hbm.1, bf16[64,512]{1,0:T(8,128)(2,1)} %vp_hbm.1, ...), custom_call_target="tpu_custom_call" | custom-call | tf_op jit(solution)/shard_map/attention_backward/pallas_call | solution.py:562
  92.2 2.4 %hand_over.1 = (bf16[1,128,4096]{2,1,0:T(8,128)(2,1)}, bf16[64,512]{1,0:T(8,128)(2,1)}, bf16[64,512]{1,0:T(8,128)(2,1)}, bf16[1,128,512]{2,1,0:T(8,128)(2,1)}, bf16[1,128,512]{2,1,0:T(8,128)(2,1)}) custom-call(bf16[1,128,4096]{2,1,0:T(8,128)(2,1)} %get-tuple-element.10.refs_0_, bf16[64,512]{1,0:T(8,128)(2,1)} %get-tuple-element.11.refs_1_, ...), custom_call_target="tpu_custom_call" | custom-call | tf_op jit(solution)/shard_map/hand_over/pallas_call | solution.py:618

commit v4 on v3

--- a/solution.py
+++ b/solution.py
@@ -417,8 +417,6 @@
             def _():
                 gather_a(3)
 
-            transpose_keys(h, pre, win, kt, h)
-
         scores(h, half, qt, dot, pre, win, bias, live, s_scr, dp_scr, pb, dsb, h)
 
         @pl.when(half == 0)
@@ -464,15 +462,19 @@
                 reduce_c(h - 3)
 
     total_d(2)
+    transpose_keys(0, pre, win, kt, 0)
     query_terms(0, kt, dsb, q_v, 0)
     reduce_b(2)
+    transpose_keys(1, pre, win, kt, 1)
     query_terms(1, kt, dsb, q_v, 1)
+    transpose_keys(2, pre, win, kt, 2)
     query_terms(2, kt, dsb, q_v, 2)
     total_e(2)
+    total_d(3)
+    transpose_keys(3, pre, win, kt, 3)
     query_terms(3, kt, dsb, q_v, 3)
     store_q = pltpu.make_async_copy(q_v, dq_hbm.at[0], local.at[12])
     store_q.start()
-    total_d(3)
     total_f(1)
     for o in three:
         for h in range(2):

time: 94.7 us -> 93.7 us (0.989)
  no operation moved by 1% of the time
where the time goes in v4:
time: 93.7 us; the launch traced here: 93.6 us
  Pallas kernels  93 us (99%)
    pallas_call x1, Pallas kernels, shards(): pl.pallas_call(kernel, out_shape=(jax.ShapeDtypeStruct(q.shape, bf), jax....  90.6 us
    pallas_call x1, Pallas kernels, shards(): pl.pallas_call(hand_over, out_shape=tuple((jax.ShapeDtypeStruct(o.shape,...  2.35 us

profile of v4, /device:TPU:1, one launch (start us, length us, event | category | flops | bytes accessed | tf_op | source)
XLA Modules:
  0.0 93.6 jit_solution(7446736302377179488)
XLA Ops:
  0.6 90.6 %attention_backward.1 = (bf16[1,128,4096]{2,1,0:T(8,128)(2,1)}, bf16[64,512]{1,0:T(8,128)(2,1)}, bf16[64,512]{1,0:T(8,128)(2,1)}, bf16[1,128,512]{2,1,0:T(8,128)(2,1)}, bf16[1,128,512]{2,1,0:T(8,128)(2,1)}) custom-call(bf16[1,128,4096]{2,1,0:T(8,128)(2,1)} %q_hbm.1, bf16[64,512]{1,0:T(8,128)(2,1)} %kp_hbm.1, bf16[64,512]{1,0:T(8,128)(2,1)} %vp_hbm.1, ...), custom_call_target="tpu_custom_call" | custom-call | tf_op jit(solution)/shard_map/attention_backward/pallas_call | solution.py:564
  91.2 2.4 %hand_over.1 = (bf16[1,128,4096]{2,1,0:T(8,128)(2,1)}, bf16[64,512]{1,0:T(8,128)(2,1)}, bf16[64,512]{1,0:T(8,128)(2,1)}, bf16[1,128,512]{2,1,0:T(8,128)(2,1)}, bf16[1,128,512]{2,1,0:T(8,128)(2,1)}) custom-call(bf16[1,128,4096]{2,1,0:T(8,128)(2,1)} %get-tuple-element.10.refs_0_, bf16[64,512]{1,0:T(8,128)(2,1)} %get-tuple-element.11.refs_1_, ...), custom_call_target="tpu_custom_call" | custom-call | tf_op jit(solution)/shard_map/hand_over/pallas_call | solution.py:620
